TPU v7x, 256 devices: a whole 4x4x8 slice. The times are simulated.
256 devices in a mesh: seq: 64 (over y, x_lo, z), rep: 4 (over x_hi, core).
Axes of the slice: x: 4 (x_hi: 2, x_lo: 2; x = x_hi * 2 + x_lo), y: 4, z: 8, core: 2. Of those that a mesh axis runs over, the one named last changes fastest.
Arguments:
- inputs: bfloat16 [4, 4, 4096, 1024], P('rep', None, 'seq'), may hold values from -16 to 16
- upstream: bfloat16 [4, 4, 4096, 1024], P('rep', None, 'seq'), may hold values from -6 to 6
- qkv_weight: bfloat16 [1024, 3072], P(None, 'rep'), may hold values from -1 to 1
- out_weight: bfloat16 [1024, 1024], P(None, 'rep'), may hold values from -0.1875 to 0.1875
Outputs:
- input_grad: bfloat16 [4, 4, 4096, 1024], P('rep', None, 'seq')
- qkv_grad: float32 [1024, 3072], P('seq', 'rep')
- out_grad: float32 [1024, 1024], P('seq', 'rep')
All inputs are finite; a program needn't handle non-finite values.
Results may differ from a plain program's by a relative error of at most 0.022.
The roundings to bfloat16 on the way count: a program that leaves them out, or rounds other values in their place, can miss the bound.
Values may be sent and summed in bfloat16 or wider, within the bound.
No kernel may reach another device: no remote copies, remote signals or barrier semaphores. Data moves between devices by JAX's collectives and lax.ppermute only.
A program may use at most 128 MiB of HBM per device.

v0:
```python
import jax
import jax.numpy as jnp
from jax import lax
from jax.experimental import pallas as pl
from jax.experimental.pallas import tpu as pltpu
from jax.sharding import PartitionSpec as P

D = 1024
HEADS = 16
HD = 64
WINDOW = 512
NY, NX, NZ = 4, 4, 8
BOTH = ("seq", "rep")
BF16 = jnp.bfloat16
F32 = jnp.float32
LOG2E = 1.4426950408889634
PARAMS = pltpu.CompilerParams(vmem_limit_bytes=48 * 1024 * 1024)


def flat(y, x, z, c):
    y, x, z = y % NY, x % NX, z % NZ
    return ((y * 2 + x % 2) * NZ + z) * 4 + (x // 2) * 2 + c


PLACES = [(y, x, z, c) for y in range(NY) for x in range(NX) for z in range(NZ) for c in range(2)]


def move(value, target):
    pairs = []
    for place in PLACES:
        goal = target(*place)
        if goal is not None:
            pairs.append((flat(*place), flat(*goal)))
    return lax.ppermute(value, BOTH, pairs)


def other_core(value):
    return move(value, lambda y, x, z, c: (y, x, z, 1 - c))


def mm(a, b, ca, cb):
    return lax.dot_general(a, b, (((ca,), (cb,)), ((), ())), preferred_element_type=F32)


def attention_kernel(bias_ref, q_ref, g_ref, k_ref, v_ref, dq_ref, att_ref, dk_ref, dv_ref):
    size = 256
    bias = bias_ref[0, 0]
    low = lax.broadcasted_iota(jnp.int32, (1, 2 * HD), 1) < HD
    upper = (
        lax.broadcasted_iota(jnp.int32, (size, size), 0) > lax.broadcasted_iota(jnp.int32, (size, size), 1)
    )
    factor = LOG2E * HD ** -0.5
    tiles = [slice(i * size, (i + 1) * size) for i in range(4)]
    keys = [k_ref[tile, :] for tile in tiles]
    vals = [v_ref[tile, :] for tile in tiles]
    keys_t = [k.T for k in keys]
    vals_t = [v.T for v in vals]
    dk = [None] * 4
    dv = [None] * 4

    def add(total, index, term):
        total[index] = term if total[index] is None else total[index] + term

    for block in range(2):
        rows = tiles[block]
        q_pair = q_ref[rows, :]
        g_pair = g_ref[rows, :]
        g_t = g_pair.T.astype(F32)
        dq_t = []
        for head in range(2):
            mine = low if head == 0 else jnp.logical_not(low)
            lanes = slice(head * HD, (head + 1) * HD)
            q = jnp.where(mine, q_pair, jnp.zeros_like(q_pair))
            g = jnp.where(mine, g_pair, jnp.zeros_like(g_pair))
            s0, s1, s2 = [mm(keys[block + i], q, 1, 1) for i in range(3)]
            edge = jnp.where(upper, s0 + bias, s2)
            if block == 0:
                s1 = s1 + bias
            top = jnp.maximum(
                jnp.max(edge, axis=0, keepdims=True), jnp.max(s1, axis=0, keepdims=True)
            )
            edge = jnp.exp2((edge - top) * factor)
            full = jnp.exp2((s1 - top) * factor)
            scale = 1.0 / (jnp.sum(edge, axis=0, keepdims=True) + jnp.sum(full, axis=0, keepdims=True))
            edge = edge * scale
            full = full * scale
            p0 = jnp.where(upper, edge, 0.0).astype(BF16)
            p1 = full.astype(BF16)
            p2 = jnp.where(upper, 0.0, edge).astype(BF16)
            att = (
                mm(vals_t[block][lanes], p0, 1, 0)
                + mm(vals_t[block + 1][lanes], p1, 1, 0)
                + mm(vals_t[block + 2][lanes], p2, 1, 0)
            )
            delta = jnp.sum(g_t[lanes] * att, axis=0, keepdims=True)
            att_ref[lanes, rows] = att.astype(BF16)
            d0, d1, d2 = [mm(vals[block + i], g, 1, 1) for i in range(3)]
            d_edge = edge * (jnp.where(upper, d0, d2) - delta)
            z0 = jnp.where(upper, d_edge, 0.0).astype(BF16)
            z1 = (full * (d1 - delta)).astype(BF16)
            z2 = jnp.where(upper, 0.0, d_edge).astype(BF16)
            dq_t.append(
                mm(keys_t[block][lanes], z0, 1, 0)
                + mm(keys_t[block + 1][lanes], z1, 1, 0)
                + mm(keys_t[block + 2][lanes], z2, 1, 0)
            )
            for i, (p, z) in enumerate(((p0, z0), (p1, z1), (p2, z2))):
                add(dv, block + i, mm(p, g, 1, 0))
                add(dk, block + i, mm(z, q, 1, 0))
        dq = jnp.concatenate(dq_t, axis=0) * (HD ** -0.5)
        dq_ref[rows, :] = dq.T.astype(BF16)
    for i, tile in enumerate(tiles):
        dk_ref[tile, :] = (dk[i] * (HD ** -0.5)).astype(BF16)
        dv_ref[tile, :] = dv[i].astype(BF16)


def attention(bias, qkv, g):
    tokens, width = g.shape
    pairs = width // (2 * HD)
    own = pl.BlockSpec((tokens, 2 * HD), lambda i: (0, i))
    long = pl.BlockSpec((2 * tokens, 2 * HD), lambda i: (0, i))
    return pl.pallas_call(
        attention_kernel,
        grid=(pairs,),
        in_specs=[
            pl.BlockSpec(memory_space=pltpu.SMEM),
            pl.BlockSpec((tokens, 2 * HD), lambda i: (1, i)),
            own,
            pl.BlockSpec((2 * tokens, 2 * HD), lambda i: (0, pairs + i)),
            pl.BlockSpec((2 * tokens, 2 * HD), lambda i: (0, 2 * pairs + i)),
        ],
        out_specs=[own, pl.BlockSpec((2 * HD, tokens), lambda i: (i, 0)), long, long],
        out_shape=[
            jax.ShapeDtypeStruct((tokens, width), BF16),
            jax.ShapeDtypeStruct((width, tokens), BF16),
            jax.ShapeDtypeStruct((2 * tokens, width), BF16),
            jax.ShapeDtypeStruct((2 * tokens, width), BF16),
        ],
        compiler_params=PARAMS,
        cost_estimate=pl.CostEstimate(
            flops=16 * 768 * 256 * 64 * 12, bytes_accessed=6 * 1024 * 1024, transcendentals=16 * 512 * 256
        ),
    )(bias, qkv, g, qkv, qkv)


def token_grad_kernel(*refs):
    out_ref = refs[-1]
    pairs = [(refs[2 * i], refs[2 * i + 1]) for i in range(len(refs) // 2)]
    for half in range(2):
        cols = slice(half * 512, (half + 1) * 512)
        acc = None
        for grad_ref, weight_ref in pairs:
            term = mm(grad_ref[...], weight_ref[cols, :], 1, 1)
            acc = term if acc is None else acc + term
        out_ref[half] = acc.astype(BF16)


def token_grad(rows, weight, dq, dk, dv):
    whole = pl.BlockSpec((512, 512), lambda i: (0, 0))
    tokens = pl.BlockSpec((512, 512), lambda i: (rows, 0))

    def cols(which):
        return pl.BlockSpec((1024, 512), lambda i: (0, which))

    specs, args = [], []
    if dq is not None:
        specs, args = [whole, cols(0)], [dq, weight]
    return pl.pallas_call(
        token_grad_kernel,
        grid=(1,),
        in_specs=specs + [tokens, cols(1), tokens, cols(2)],
        out_specs=pl.BlockSpec((2, 512, 512), lambda i: (0, 0, 0)),
        out_shape=jax.ShapeDtypeStruct((2, 512, 512), BF16),
        compiler_params=PARAMS,
        cost_estimate=pl.CostEstimate(
            flops=2 * 512 * 1024 * 512 * (len(args) // 2 + 2), bytes_accessed=5 << 20, transcendentals=0
        ),
    )(*args, dk, weight, dv, weight)


def weight_grad_a_kernel(src_ref, dq_ref, dk_ref, dv_ref, out_ref):
    for y in range(4):
        rows = slice(y * 256, (y + 1) * 256)
        out_ref[y, :, :256] = mm(src_ref[rows, 512:], dq_ref[...], 1, 0).astype(BF16)
        out_ref[y, :, 256:768] = mm(src_ref[rows, :], dk_ref[...], 1, 0).astype(BF16)
        out_ref[y, :, 768:] = mm(src_ref[rows, :], dv_ref[...], 1, 0).astype(BF16)


def weight_grad_c_kernel(src_ref, dq_ref, dv_ref, att_ref, cot_ref, out_ref):
    for y in range(4):
        rows = slice(y * 256, (y + 1) * 256)
        parts = (mm(src_ref[rows, 512:], dq_ref[...], 1, 0), mm(src_ref[rows, :], dv_ref[...], 1, 0))
        for hi in range(2):
            for lo in range(2):
                piece = parts[hi][lo * 128:(lo + 1) * 128].astype(BF16)
                out_ref[2 * hi + lo, y * 128:(y + 1) * 128, :] = piece
    for group in range(2):
        for rep in range(4):
            part = mm(att_ref[group * 256:(group + 1) * 256, :], cot_ref[:, rep * 256:(rep + 1) * 256], 1, 0)
            start = 512 + (2 * (rep % 2) + group) * 128
            for lo in range(2):
                piece = part[lo * 128:(lo + 1) * 128].astype(BF16)
                out_ref[2 * (rep // 2) + lo, start:start + 128, :] = piece


def weight_grads_a(src_t, dq, dk, dv):
    return pl.pallas_call(
        weight_grad_a_kernel,
        grid=(1,),
        in_specs=[
            pl.BlockSpec((1024, 1024), lambda i: (0, 0)),
            pl.BlockSpec((512, 256), lambda i: (0, 0)),
            pl.BlockSpec((1024, 512), lambda i: (0, 0)),
            pl.BlockSpec((1024, 256), lambda i: (0, 1)),
        ],
        out_specs=pl.BlockSpec((4, 256, 1024), lambda i: (0, 0, 0)),
        out_shape=jax.ShapeDtypeStruct((4, 256, 1024), BF16),
        compiler_params=PARAMS,
        cost_estimate=pl.CostEstimate(flops=2 * 1024 * 1024 * 900, bytes_accessed=6 << 20, transcendentals=0),
    )(src_t, dq, dk, dv)


def weight_grads_c(src_t, dq, dv, att_t, cot):
    return pl.pallas_call(
        weight_grad_c_kernel,
        grid=(1,),
        in_specs=[
            pl.BlockSpec((1024, 1024), lambda i: (0, 0)),
            pl.BlockSpec((512, 256), lambda i: (0, 1)),
            pl.BlockSpec((1024, 256), lambda i: (0, 0)),
            pl.BlockSpec((512, 512), lambda i: (0, 0)),
            pl.BlockSpec((512, 1024), lambda i: (0, 0)),
        ],
        out_specs=pl.BlockSpec((4, 1024, 256), lambda i: (0, 0, 0)),
        out_shape=jax.ShapeDtypeStruct((4, 1024, 256), BF16),
        compiler_params=PARAMS,
        cost_estimate=pl.CostEstimate(flops=2 * 1024 * 1024 * 640, bytes_accessed=6 << 20, transcendentals=0),
    )(src_t, dq, dv, att_t, cot)


def regroup(value, names, groups):
    return lax.all_to_all(value, names, 0, 0, axis_index_groups=groups, tiled=True)


def total(value, parts):
    return jnp.sum(value.reshape((parts,) + (-1,) + value.shape[1:]).astype(F32), axis=0)


def spread_sum(value, here, target):
    came = []
    for step in (1, 3, 2):
        chunk = lax.dynamic_index_in_dim(value, lax.rem(here + step, 4), 0, keepdims=False)
        came.append(move(chunk, lambda y, x, z, c, step=step: target(step, y, x, z, c)))
    mine = lax.dynamic_index_in_dim(value, here, 0, keepdims=False)
    return mine.astype(F32) + came[0].astype(F32) + came[1].astype(F32) + came[2].astype(F32)


def along_y(step, y, x, z, c):
    return (y + step, x, z, c)


def along_x(step, y, x, z, c):
    return (y, x + step, z, c)


ALL_Y, ALL_X, ALL_Z, ALL_C = range(NY), range(NX), range(NZ), range(2)
Z_GROUPS = [[ring * NZ + z for z in ALL_Z] for ring in range(8)]
Y_GROUPS = [[(y * 2 + xl) * NZ + z for y in ALL_Y] for xl in range(2) for z in ALL_Z]
XC_GROUPS = [
    [flat(y, 2 * xh + xl, z, c) for xl in range(2) for xh in range(2) for c in ALL_C] for y in ALL_Y for z in ALL_Z
]


def next_ring(y, x, z, c):
    ring = 2 * y + x % 2 + 1
    return None if ring == 8 else (ring // 2, (x // 2) * 2 + ring % 2, z, c)


def last_ring(y, x, z, c):
    ring = 2 * y + x % 2 - 1
    return None if ring < 0 else (ring // 2, (x // 2) * 2 + ring % 2, z, c)


def body(inputs, upstream, qkv_weight, out_weight):
    at = lax.axis_index("seq")
    rep = lax.axis_index("rep")
    core = lax.rem(rep, 2)
    ring = at // NZ
    y = ring // 2
    x = 2 * (rep // 2) + lax.rem(ring, 2)
    first = core == 0
    left = rep // 2 == 0

    def in_order(mine, other, axis):
        return jnp.concatenate([jnp.where(first, mine, other), jnp.where(first, other, mine)], axis=axis)

    def groups_of(out, core):
        out = out.reshape(4, 256, 256)
        return jnp.concatenate(
            [lax.dynamic_index_in_dim(out, core, 0, False), lax.dynamic_index_in_dim(out, 2 + core, 0, False)],
            axis=0,
        )

    def across(y, x, z, c):
        return (y, 3 - x, z, c)

    near_give = jnp.concatenate([qkv_weight[:, 256:512], groups_of(out_weight, 1 - core)], axis=0)
    near = jnp.concatenate(
        [qkv_weight[:, :256], qkv_weight[:, 512:], groups_of(out_weight, core)], axis=0
    )
    far_give = move(near_give, across)
    far = move(near, across)
    near_swap = other_core(near_give)
    far_swap = other_core(far_give)

    def to_chips(tokens):
        low, high = tokens[..., :512], tokens[..., 512:]
        other = other_core(jnp.where(first, high, low))
        mixed = in_order(jnp.where(first, low, high), other, 0)
        return regroup(mixed, "seq", Z_GROUPS).reshape(NZ * 64, 512)

    src = to_chips(inputs[0])
    halo = move(src, next_ring)
    cot = to_chips(upstream[0])
    src = jnp.concatenate([halo, src], axis=0)
    src = in_order(src, other_core(src), 1)
    cot = in_order(cot, other_core(cot), 1)

    lo, hi = jnp.where(left, near, far), jnp.where(left, far, near)
    lo_swap, hi_swap = jnp.where(left, near_swap, far_swap), jnp.where(left, far_swap, near_swap)
    weight = jnp.concatenate(
        [
            jnp.where(first, lo[:1024], lo_swap[:1024]),
            jnp.where(first, lo[1024:2048], lo[:1024]),
            jnp.where(first, lo_swap[:1024], lo[1024:2048]),
            jnp.where(first, hi[:1024], hi_swap[:1024]),
            jnp.where(first, hi[1024:2048], hi[:1024]),
            jnp.where(first, hi_swap[:1024], hi[1024:2048]),
        ],
        axis=1,
    )
    weight_o = jnp.concatenate(
        [in_order(lo[2048:], lo_swap[1024:], 1), in_order(hi[2048:], hi_swap[1024:], 1)], axis=1
    )
    src_t = src.T

    qkv = mm(src, weight, 1, 0).astype(BF16)
    g = mm(cot, weight_o, 1, 1).astype(BF16)
    bias = jnp.where(ring == 0, -jnp.inf, 0.0).astype(F32).reshape(1, 1)
    dq, att_t, dk, dv = attention(bias, qkv, g)

    def core_sum(value):
        mine = lax.dynamic_index_in_dim(value, core, 0, keepdims=False)
        other = other_core(lax.dynamic_index_in_dim(value, 1 - core, 0, keepdims=False))
        return mine.astype(F32) + other.astype(F32)

    ig_halo = token_grad(0, weight, None, dk, dv)
    returned = move(core_sum(ig_halo).astype(BF16), last_ring)
    dq, dk, dv, ig_halo = lax.optimization_barrier((dq, dk, dv, ig_halo))

    part_a = weight_grads_a(src_t, dq, dk, dv)
    dq, dk, dv, part_a = lax.optimization_barrier((dq, dk, dv, part_a))
    part_a = total(regroup(part_a, "seq", Y_GROUPS), NY)[0].astype(BF16)

    part_c = weight_grads_c(src_t, dq, dv, att_t, cot)
    dq, dk, dv, part_c = lax.optimization_barrier((dq, dk, dv, part_c))
    part_c = spread_sum(part_c, x, along_x).astype(BF16)

    ig = core_sum(token_grad(1, weight, dq, dk, dv))
    ig = (ig + returned.astype(F32)).astype(BF16).reshape(8, 64, 512)
    ig = regroup(ig, "seq", Z_GROUPS).reshape(2, 4, 64, 512)
    kept = lax.dynamic_index_in_dim(ig, core, 0, keepdims=False)
    came = other_core(lax.dynamic_index_in_dim(ig, 1 - core, 0, keepdims=False))
    input_grad = in_order(kept, came, -1)[None]

    part_a = part_a.reshape(2, 128, 4, 256).transpose(0, 2, 1, 3).reshape(8, 128, 256)
    part_a = regroup(part_a, BOTH, XC_GROUPS).reshape(4, 2, 128, 256)
    part_a = jnp.sum(part_a.astype(F32), axis=0).astype(BF16)

    part_o = part_c[512:].reshape(2, 2, 1, 128, 256)
    mine = lax.dynamic_index_in_dim(part_o, core, 0, keepdims=False)
    other = other_core(lax.dynamic_index_in_dim(part_o, 1 - core, 0, keepdims=False))
    part_o = in_order(mine, other, 1).reshape(4, 128, 256)
    part_c = jnp.concatenate([part_c[:512].reshape(4, 128, 256), part_o], axis=1)
    part_c = spread_sum(part_c, y, along_y).astype(BF16).reshape(2, 128, 256)

    last = jnp.concatenate([part_a, part_c], axis=0).reshape(4, 8, 16, 256).transpose(1, 0, 2, 3)
    last = jnp.sum(regroup(last, "seq", Z_GROUPS).astype(F32), axis=0)
    qkv_grad = jnp.where(
        first,
        jnp.concatenate([last[0], last[1], last[2]], axis=1),
        jnp.concatenate([last[2], last[0], last[1]], axis=1),
    )
    return input_grad, qkv_grad, last[3]


def solution(mesh):
    return jax.shard_map(
        body,
        mesh=mesh,
        in_specs=(
            P("rep", None, "seq", None),
            P("rep", None, "seq", None),
            P(None, "rep"),
            P(None, "rep"),
        ),
        out_specs=(P("rep", None, "seq", None), P("seq", "rep"), P("seq", "rep")),
        check_vma=False,
    )
```

profile of v0, /device:TPU:24, one launch (start us, length us, event | category | flops | bytes accessed | tf_op | source)
XLA Modules:
  0.0 220.1 jit_solution(10159851261545424870)
XLA Ops:
  0.6 1.1 broadcast_select_fusion.18
  1.8 1.8 broadcast_select_fusion.14
  3.6 0.5 collective-permute-start.7
  4.1 1.1 broadcast_select_fusion.17
  5.2 0.8 pad_maximum_fusion.6
  6.0 8.6 %all-to-all-start = ((bf16[8,64,512]{2,1,0:T(8,128)(2,1)}), bf16[8,64,512]{2,1,0:T(8,128)(2,1)S(1)}, u32[]{:S(2)}, u32[]{:S(2)}) async-start(bf16[8,64,512]{2,1,0:T(8,128)(2,1)} %pad_maximum_fusion.6), calls=%async_computation | async-start | bytes 1048576 | tf_op jit(solution)/shard_map/all_to_all | solution.py:242
  14.6 1.5 fusion.27
  16.1 0.7 dynamic-slice_bitcast_fusion.10
  16.8 1.2 pad_maximum_fusion.2
  18.0 2.8 %collective-permute-start.3 = (bf16[2560,256]{1,0:T(8,128)(2,1)}, bf16[2560,256]{1,0:T(8,128)(2,1)}, u32[]{:S(2)}, u32[]{:S(2)}) collective-permute-start(bf16[2560,256]{1,0:T(8,128)(2,1)} %pad_maximum_fusion.2), channel_id=1, source_target_pairs={{0,34},{1,35},{4,38},{5,39},{8,42},{9,43},{12,46},{13,47},{16,50},... | collective-permute-start | bytes 3932168 | tf_op jit(solution)/shard_map/ppermute | solution.py:34
  20.7 1.0 broadcast_select_fusion.13
  21.7 0.8 pad_maximum_fusion.7
  22.6 9.7 %all-to-all-done = bf16[8,64,512]{2,1,0:T(8,128)(2,1)S(1)} async-done(((bf16[8,64,512]{2,1,0:T(8,128)(2,1)}), bf16[8,64,512]{2,1,0:T(8,128)(2,1)S(1)}, u32[]{:S(2)}, u32[]{:S(2)}) %all-to-all-start) | async-done | bytes 524320 | tf_op jit(solution)/shard_map/all_to_all | solution.py:242
  32.3 3.5 %all-to-all-start.1 = ((bf16[8,64,512]{2,1,0:T(8,128)(2,1)}), bf16[8,64,512]{2,1,0:T(8,128)(2,1)S(1)}, u32[]{:S(2)}, u32[]{:S(2)}) async-start(bf16[8,64,512]{2,1,0:T(8,128)(2,1)} %pad_maximum_fusion.7), calls=%async_computation.1 | async-start | bytes 1048576 | tf_op jit(solution)/shard_map/all_to_all | solution.py:242
  35.8 1.9 pad_maximum_fusion.5
  37.6 2.8 %collective-permute-start.5 = (bf16[1536,256]{1,0:T(8,128)(2,1)}, bf16[1536,256]{1,0:T(8,128)(2,1)}, u32[]{:S(2)}, u32[]{:S(2)}) collective-permute-start(bf16[1536,256]{1,0:T(8,128)(2,1)} %pad_maximum_fusion.5), channel_id=1, source_target_pairs={{0,34},{1,35},{4,38},{5,39},{8,42},{9,43},{12,46},{13,47},{16,50},... | collective-permute-start | bytes 2359304 | tf_op jit(solution)/shard_map/ppermute | solution.py:34
  40.4 26.4 %collective-permute-done.5 = bf16[1536,256]{1,0:T(8,128)(2,1)} collective-permute-done((bf16[1536,256]{1,0:T(8,128)(2,1)}, bf16[1536,256]{1,0:T(8,128)(2,1)}, u32[]{:S(2)}, u32[]{:S(2)}) %collective-permute-start.5) | collective-permute-done | bytes 786464 | tf_op jit(solution)/shard_map/ppermute | solution.py:34
  67.0 2.2 collective-permute-start.1
  69.5 1.8 broadcast_select_fusion
  71.4 1.5 broadcast_select_fusion.4
  73.4 10.7 %collective-permute-done.1 = bf16[512,512]{0,1:T(8,128)(2,1)S(1)} collective-permute-done((bf16[512,512]{0,1:T(8,128)(2,1)S(1)}, bf16[512,512]{0,1:T(8,128)(2,1)S(1)}, u32[]{:S(2)}, u32[]{:S(2)}) %collective-permute-start.1) | collective-permute-done | bytes 524320 | tf_op jit(solution)/shard_map/ppermute | solution.py:34
  85.1 0.7 convolution_convert_fusion.1.g_ref
  85.8 1.4 collective-permute-done.2
  87.2 0.5 broadcast_select_fusion.3
  87.7 1.6 fusion.src_ref
  89.3 4.9 %convolution_convert_fusion.q_ref.k_ref.v_ref = bf16[1024,1536]{1,0:T(8,128)(2,1)} fusion(bf16[1024,1536]{1,0:T(8,128)(2,1)S(1)} %select_dynamic-update-slice_fusion.refs_1_.refs_3_.refs_5_, bf16[1024,512]{0,1:T(8,128)(2,1)S(1)} %get-tuple-element.43, bf16[1024,512]{0,1:T(8,128)(2,1)S(1)} %get-tuple-element.42), kind=kOutput, calls=%fused_computation | convolution fusion | flops 3226992640 | bytes 8388608 | tf_op jit(solution)/shard_map/dot_general | solution.py:42
  94.1 17.4 %shard_map.67 = (bf16[512,512]{1,0:T(8,128)(2,1)S(1)}, bf16[512,512]{1,0:T(8,128)(2,1)S(1)}, bf16[1024,512]{1,0:T(8,128)(2,1)S(1)}, bf16[1024,512]{1,0:T(8,128)(2,1)S(1)}) custom-call(f32[1,1]{1,0:T(1,128)} %bitcast.bias_ref, bf16[1024,1536]{1,0:T(8,128)(2,1)} %convolution_convert_fusion.q_ref.k_ref.v_ref, ...), custom_call_target="tpu_custom_call" | custom-call | flops 2415919104 | bytes 6291456 | tf_op jit(solution)/shard_map/pallas_call | solution.py:122
  111.6 0.8 copy-done.8
  112.4 3.4 %shard_map.68 = bf16[2,512,512]{2,1,0:T(8,128)(2,1)S(1)} custom-call(bf16[1024,512]{1,0:T(8,128)(2,1)S(1)} %get-tuple-element.29.refs_0_.dk_ref.refs_2_, bf16[1024,1536]{1,0:T(8,128)(2,1)} %copy-done.10, bf16[1024,512]{1,0:T(8,128)(2,1)S(1)} %get-tuple-element.30.refs_2_.dv_ref.refs_4_, bf16[1024,1536]{1,0:T(8,128)(2,1)} %copy-done.10), custom_call_target="tpu_custom_call" | custom-call | flops 1073741824 | bytes 5242880 | tf_op jit(solution)/shard_map/pallas_call | solution.py:168
  115.8 1.0 copy-done.4
  116.8 0.8 dynamic-slice_bitcast_fusion.3
  117.8 5.0 %shard_map.69 = bf16[4,256,1024]{2,1,0:T(8,128)(2,1)} custom-call(bf16[1024,1024]{1,0:T(8,128)(2,1)} %fusion.src_ref, bf16[512,512]{1,0:T(8,128)(2,1)S(1)} %get-tuple-element.28.dq_ref.refs_0_, bf16[1024,512]{1,0:T(8,128)(2,1)S(1)} %get-tuple-element.29.refs_0_.dk_ref.refs_2_, bf16[1024,512]{1,0:T(8,128)(2,1)S(1)} %get-tuple-element.30.refs_2_.dv_ref.refs_4_), custom_call_target="tpu_custom_call" | custom-call | flops 1887436800 | bytes 6291456 | tf_op jit(solution)/shard_map/pallas_call | solution.py:207
  122.7 4.7 %all-to-all-start.3 = ((bf16[4,256,1024]{2,1,0:T(8,128)(2,1)}), bf16[4,256,1024]{2,1,0:T(8,128)(2,1)}, u32[]{:S(2)}, u32[]{:S(2)}) async-start(bf16[4,256,1024]{2,1,0:T(8,128)(2,1)} %shard_map.69), calls=%async_computation.3 | async-start | bytes 4194304 | tf_op jit(solution)/shard_map/all_to_all | solution.py:242
  127.6 0.9 copy-done.7
  128.6 3.2 %shard_map.70 = bf16[4,1024,256]{2,1,0:T(8,128)(2,1)S(1)} custom-call(bf16[1024,1024]{1,0:T(8,128)(2,1)} %fusion.src_ref, bf16[512,512]{1,0:T(8,128)(2,1)S(1)} %copy-done.7, bf16[1024,512]{1,0:T(8,128)(2,1)S(1)} %get-tuple-element.30.refs_2_.dv_ref.refs_4_, bf16[512,512]{1,0:T(8,128)(2,1)S(1)} %copy-done.9, bf16[512,1024]{1,0:T(8,128)(2,1)S(1)} %pad_maximum_fusion.4.cot_ref), custom_call_target="tpu_custom_call" | custom-call | flops 1342177280 | bytes 6291456 | tf_op jit(solution)/shard_map/pallas_call | solution.py:224
  131.9 3.8 %shard_map.71 = bf16[2,512,512]{2,1,0:T(8,128)(2,1)S(1)} custom-call(bf16[512,512]{1,0:T(8,128)(2,1)S(1)} %copy-done.7, bf16[1024,1536]{1,0:T(8,128)(2,1)} %copy-done.10, bf16[1024,512]{1,0:T(8,128)(2,1)S(1)} %copy-done.1, bf16[1024,1536]{1,0:T(8,128)(2,1)} %copy-done.10, bf16[1024,512]{1,0:T(8,128)(2,1)S(1)} %get-tuple-element.30.refs_2_.dv_ref.refs_4_, ...), custom_call_target="tpu_custom_call" | custom-call | flops 1610612736 | bytes 5242880 | tf_op jit(solution)/shard_map/pallas_call | solution.py:168
  135.7 1.0 copy-done.2
  136.6 0.8 dynamic-slice_bitcast_fusion.4
  137.8 2.0 fusion.11
  139.8 1.9 collective-permute-start.11
  141.8 1.2 dynamic-slice_bitcast_fusion.2
  143.0 3.6 %collective-permute-start.15 = (bf16[1024,256]{1,0:T(8,128)(2,1)}, bf16[1024,256]{1,0:T(8,128)(2,1)}, u32[]{:S(2)}, u32[]{:S(2)}) collective-permute-start(bf16[1024,256]{1,0:T(8,128)(2,1)} %get-tuple-element.36), channel_id=1, source_target_pairs={{0,2},{1,3},{4,6},{5,7},{8,10},{9,11},{12,14},{13,15},{16,18},{17,... | collective-permute-start | bytes 1572872 | tf_op jit(solution)/shard_map/ppermute | solution.py:34
  146.5 1.9 collective-permute-start.14
  148.6 8.2 %collective-permute-done.11 = bf16[512,512]{1,0:T(8,128)(2,1)} collective-permute-done((bf16[512,512]{1,0:T(8,128)(2,1)}, bf16[512,512]{1,0:T(8,128)(2,1)}, u32[]{:S(2)}, u32[]{:S(2)}) %collective-permute-start.11) | collective-permute-done | bytes 524320 | tf_op jit(solution)/shard_map/ppermute | solution.py:34
  156.8 2.2 fusion.13
  159.0 6.9 %all-to-all-start.2 = ((bf16[8,64,512]{2,1,0:T(8,128)(2,1)}), bf16[8,64,512]{2,1,0:T(8,128)(2,1)S(1)}, u32[]{:S(2)}, u32[]{:S(2)}) async-start(bf16[8,64,512]{2,1,0:T(8,128)(2,1)} %bitcast.92), calls=%async_computation.2 | async-start | bytes 1048576 | tf_op jit(solution)/shard_map/all_to_all | solution.py:242
  165.9 3.7 %collective-permute-done.15 = bf16[1024,256]{1,0:T(8,128)(2,1)} collective-permute-done((bf16[1024,256]{1,0:T(8,128)(2,1)}, bf16[1024,256]{1,0:T(8,128)(2,1)}, u32[]{:S(2)}, u32[]{:S(2)}) %collective-permute-start.15) | collective-permute-done | bytes 524320 | tf_op jit(solution)/shard_map/ppermute | solution.py:34
  169.6 9.0 %collective-permute-done.14 = bf16[1024,256]{1,0:T(8,128)(2,1)} collective-permute-done((bf16[1024,256]{1,0:T(8,128)(2,1)}, bf16[1024,256]{1,0:T(8,128)(2,1)}, u32[]{:S(2)}, u32[]{:S(2)}) %collective-permute-start.14) | collective-permute-done | bytes 524320 | tf_op jit(solution)/shard_map/ppermute | solution.py:34
  178.6 1.6 fusion.10
  180.4 1.3 collective-permute-done.16
  181.8 2.0 reduce_sum.33
  183.8 0.4 convert_element_type.92
  184.2 0.9 copy.34
  185.1 6.0 %all-to-all-start.4 = ((bf16[8,128,256]{2,1,0:T(8,128)(2,1)}), bf16[8,128,256]{2,1,0:T(8,128)(2,1)S(1)}, u32[]{:S(2)}, u32[]{:S(2)}) async-start(bf16[8,128,256]{2,1,0:T(8,128)(2,1)} %bitcast.21), calls=%async_computation.4 | async-start | bytes 1048576 | tf_op jit(solution)/shard_map/all_to_all | solution.py:242
  191.1 2.8 %collective-permute-start.19 = (bf16[256,256]{1,0:T(8,128)(2,1)S(1)}, bf16[256,256]{1,0:T(8,128)(2,1)S(1)}, u32[]{:S(2)}, u32[]{:S(2)}) collective-permute-start(bf16[256,256]{1,0:T(8,128)(2,1)S(1)} %get-tuple-element.59), channel_id=1, source_target_pairs={{0,128},{1,129},{4,132},{5,133},{8,136},{9,137},{12,140},{13,141},... | collective-permute-start | bytes 393224 | tf_op jit(solution)/shard_map/ppermute | solution.py:34
  193.9 3.2 %collective-permute-start.17 = (bf16[256,256]{1,0:T(8,128)(2,1)S(1)}, bf16[256,256]{1,0:T(8,128)(2,1)S(1)}, u32[]{:S(2)}, u32[]{:S(2)}) collective-permute-start(bf16[256,256]{1,0:T(8,128)(2,1)S(1)} %get-tuple-element.57), channel_id=1, source_target_pairs={{0,64},{1,65},{4,68},{5,69},{8,72},{9,73},{12,76},{13,77},{16,80},... | collective-permute-start | bytes 393224 | tf_op jit(solution)/shard_map/ppermute | solution.py:34
  197.3 1.8 collective-permute-done.19
  199.0 2.4 %collective-permute-done.18 = bf16[256,256]{1,0:T(8,128)(2,1)S(1)} collective-permute-done((bf16[256,256]{1,0:T(8,128)(2,1)S(1)}, bf16[256,256]{1,0:T(8,128)(2,1)S(1)}, u32[]{:S(2)}, u32[]{:S(2)}) %collective-permute-start.18) | collective-permute-done | bytes 131104 | tf_op jit(solution)/shard_map/ppermute | solution.py:34
  201.6 0.7 copy.35
  202.4 4.4 %all-to-all-start.5 = ((bf16[8,4,16,256]{3,2,1,0:T(8,128)(2,1)}), bf16[8,4,16,256]{3,2,1,0:T(8,128)(2,1)S(1)}, u32[]{:S(2)}, u32[]{:S(2)}) async-start(bf16[8,4,16,256]{3,2,1,0:T(8,128)(2,1)} %copy.35), calls=%async_computation.5 | async-start | bytes 524288 | tf_op jit(solution)/shard_map/all_to_all | solution.py:242
  206.8 0.9 maximum_bitcast_fusion
  207.7 11.1 %all-to-all-done.5 = bf16[8,4,16,256]{3,2,1,0:T(8,128)(2,1)S(1)} async-done(((bf16[8,4,16,256]{3,2,1,0:T(8,128)(2,1)}), bf16[8,4,16,256]{3,2,1,0:T(8,128)(2,1)S(1)}, u32[]{:S(2)}, u32[]{:S(2)}) %all-to-all-start.5) | async-done | bytes 262176 | tf_op jit(solution)/shard_map/all_to_all | solution.py:242
  218.9 0.6 slice_bitcast_fusion
  219.5 0.6 maximum_select_fusion
  (70 shorter events, 3.7 us)
Async XLA Ops:
  1.7 2.4 %collective-permute-start = (bf16[4,64,512]{2,1,0:T(8,128)(2,1)S(1)}, bf16[4,64,512]{2,1,0:T(8,128)(2,1)S(1)}, u32[]{:S(2)}, u32[]{:S(2)}) collective-permute-start(bf16[4,64,512]{2,1,0:T(8,128)(2,1)S(1)} %broadcast_select_fusion.18), channel_id=1, source_target_pairs={{0,1},{1,0},{4,5},{5,4},{8,9},{9,8},{12,13},{13,12},{16,17},{17,16... | collective-permute-start | bytes 786440 | tf_op jit(solution)/shard_map/ppermute | solution.py:34
  3.6 17.2 %collective-permute-start.7 = (bf16[4,64,512]{2,1,0:T(8,128)(2,1)}, bf16[4,64,512]{2,1,0:T(8,128)(2,1)}, u32[]{:S(2)}, u32[]{:S(2)}) collective-permute-start(bf16[4,64,512]{2,1,0:T(8,128)(2,1)} %broadcast_select_fusion.14), channel_id=1, source_target_pairs={{0,1},{1,0},{4,5},{5,4},{8,9},{9,8},{12,13},{13,12},{16,17},{17,16... | collective-permute-start | bytes 786440 | tf_op jit(solution)/shard_map/ppermute | solution.py:34
  6.0 10.1 %copy-start.12 = (bf16[1024,256]{1,0:T(8,128)(2,1)S(1)}, bf16[1024,256]{1,0:T(8,128)(2,1)}, u32[]{:S(2)}) copy-start(bf16[1024,256]{1,0:T(8,128)(2,1)} %param.7) | copy-start | bytes 1572868
  6.0 26.3 %all-to-all-start = ((bf16[8,64,512]{2,1,0:T(8,128)(2,1)}), bf16[8,64,512]{2,1,0:T(8,128)(2,1)S(1)}, u32[]{:S(2)}, u32[]{:S(2)}) async-start(bf16[8,64,512]{2,1,0:T(8,128)(2,1)} %pad_maximum_fusion.6), calls=%async_computation | async-start | bytes 1048576 | tf_op jit(solution)/shard_map/all_to_all | solution.py:242
  16.1 4.7 %copy-start.11 = (bf16[1,4,64,1024]{3,2,1,0:T(8,128)(2,1)S(1)}, bf16[1,4,64,1024]{3,2,1,0:T(8,128)(2,1)}, u32[]{:S(2)}) copy-start(bf16[1,4,64,1024]{3,2,1,0:T(8,128)(2,1)} %param.5) | copy-start | bytes 1572868
  18.0 51.6 %collective-permute-start.3 = (bf16[2560,256]{1,0:T(8,128)(2,1)}, bf16[2560,256]{1,0:T(8,128)(2,1)}, u32[]{:S(2)}, u32[]{:S(2)}) collective-permute-start(bf16[2560,256]{1,0:T(8,128)(2,1)} %pad_maximum_fusion.2), channel_id=1, source_target_pairs={{0,34},{1,35},{4,38},{5,39},{8,42},{9,43},{12,46},{13,47},{16,50},... | collective-permute-start | bytes 3932168 | tf_op jit(solution)/shard_map/ppermute | solution.py:34
  32.3 36.9 %all-to-all-start.1 = ((bf16[8,64,512]{2,1,0:T(8,128)(2,1)}), bf16[8,64,512]{2,1,0:T(8,128)(2,1)S(1)}, u32[]{:S(2)}, u32[]{:S(2)}) async-start(bf16[8,64,512]{2,1,0:T(8,128)(2,1)} %pad_maximum_fusion.7), calls=%async_computation.1 | async-start | bytes 1048576 | tf_op jit(solution)/shard_map/all_to_all | solution.py:242
  37.6 29.1 %collective-permute-start.5 = (bf16[1536,256]{1,0:T(8,128)(2,1)}, bf16[1536,256]{1,0:T(8,128)(2,1)}, u32[]{:S(2)}, u32[]{:S(2)}) collective-permute-start(bf16[1536,256]{1,0:T(8,128)(2,1)} %pad_maximum_fusion.5), channel_id=1, source_target_pairs={{0,34},{1,35},{4,38},{5,39},{8,42},{9,43},{12,46},{13,47},{16,50},... | collective-permute-start | bytes 2359304 | tf_op jit(solution)/shard_map/ppermute | solution.py:34
  40.4 31.0 %collective-permute-start.4 = (bf16[1536,256]{1,0:T(8,128)(2,1)}, bf16[1536,256]{1,0:T(8,128)(2,1)}, u32[]{:S(2)}, u32[]{:S(2)}) collective-permute-start(bf16[1536,256]{1,0:T(8,128)(2,1)} %pad_maximum_fusion.5), channel_id=1, source_target_pairs={{0,1},{1,0},{4,5},{5,4},{8,9},{9,8},{12,13},{13,12},{16,17},{17,16... | collective-permute-start | bytes 2359304 | tf_op jit(solution)/shard_map/ppermute | solution.py:34
  66.8 4.6 %collective-permute-start.6 = (bf16[1536,256]{1,0:T(8,128)(2,1)}, bf16[1536,256]{1,0:T(8,128)(2,1)}, u32[]{:S(2)}, u32[]{:S(2)}) collective-permute-start(bf16[1536,256]{1,0:T(8,128)(2,1)} %collective-permute-done.5), channel_id=1, source_target_pairs={{0,1},{1,0},{4,5},{5,4},{8,9},{9,8},{12,13},{13,12},{16,17},{17,16... | collective-permute-start | bytes 2359304 | tf_op jit(solution)/shard_map/ppermute | solution.py:34
  67.0 17.1 %collective-permute-start.1 = (bf16[512,512]{0,1:T(8,128)(2,1)S(1)}, bf16[512,512]{0,1:T(8,128)(2,1)S(1)}, u32[]{:S(2)}, u32[]{:S(2)}) collective-permute-start(bf16[512,512]{0,1:T(8,128)(2,1)S(1)} %copy.32), channel_id=1, source_target_pairs={{0,32},{1,33},{4,36},{5,37},{8,40},{9,41},{12,44},{13,45},{16,48},... | collective-permute-start | bytes 1572872 | tf_op jit(solution)/shard_map/ppermute | solution.py:34
  69.2 15.7 %collective-permute-start.8 = (bf16[512,512]{1,0:T(8,128)(2,1)S(1)}, bf16[512,512]{1,0:T(8,128)(2,1)S(1)}, u32[]{:S(2)}, u32[]{:S(2)}) collective-permute-start(bf16[512,512]{1,0:T(8,128)(2,1)S(1)} %bitcast.91), channel_id=1, source_target_pairs={{0,1},{1,0},{4,5},{5,4},{8,9},{9,8},{12,13},{13,12},{16,17},{17,16... | collective-permute-start | bytes 1572872 | tf_op jit(solution)/shard_map/ppermute | solution.py:34
  84.3 2.9 %collective-permute-start.2 = (bf16[1024,512]{0,1:T(8,128)(2,1)S(1)}, bf16[1024,512]{0,1:T(8,128)(2,1)S(1)}, u32[]{:S(2)}, u32[]{:S(2)}) collective-permute-start(bf16[1024,512]{0,1:T(8,128)(2,1)S(1)} %pad_maximum_fusion.3), channel_id=1, source_target_pairs={{0,1},{1,0},{4,5},{5,4},{8,9},{9,8},{12,13},{13,12},{16,17},{17,16... | collective-permute-start | bytes 3145736 | tf_op jit(solution)/shard_map/ppermute | solution.py:34
  84.8 4.4 %copy-start.10 = (bf16[1024,1536]{1,0:T(8,128)(2,1)}, bf16[1024,1536]{1,0:T(8,128)(2,1)S(1)}, u32[]{:S(2)}) copy-start(bf16[1024,1536]{1,0:T(8,128)(2,1)S(1)} %select_dynamic-update-slice_fusion.refs_1_.refs_3_.refs_5_) | copy-start | bytes 9437188
  111.6 0.8 copy-start.8
  112.4 5.3 %copy-start = (bf16[1024,512]{1,0:T(8,128)(2,1)}, bf16[1024,512]{1,0:T(8,128)(2,1)S(1)}, u32[]{:S(2)}) copy-start(bf16[1024,512]{1,0:T(8,128)(2,1)S(1)} %get-tuple-element.29.refs_0_.dk_ref.refs_2_) | copy-start | bytes 3145732
  112.4 5.3 %copy-start.6 = (bf16[512,512]{1,0:T(8,128)(2,1)}, bf16[512,512]{1,0:T(8,128)(2,1)S(1)}, u32[]{:S(2)}) copy-start(bf16[512,512]{1,0:T(8,128)(2,1)S(1)} %get-tuple-element.28.dq_ref.refs_0_) | copy-start | bytes 1572868
  115.8 1.0 copy-start.4
  117.6 20.2 %collective-permute-start.10 = (bf16[512,512]{1,0:T(8,128)(2,1)}, bf16[512,512]{1,0:T(8,128)(2,1)}, u32[]{:S(2)}, u32[]{:S(2)}) collective-permute-start(bf16[512,512]{1,0:T(8,128)(2,1)} %dynamic-slice_bitcast_fusion.3), channel_id=1, source_target_pairs={{0,1},{1,0},{4,5},{5,4},{8,9},{9,8},{12,13},{13,12},{16,17},{17,16... | collective-permute-start | bytes 1572872 | tf_op jit(solution)/shard_map/ppermute | solution.py:34
  122.7 36.2 %all-to-all-start.3 = ((bf16[4,256,1024]{2,1,0:T(8,128)(2,1)}), bf16[4,256,1024]{2,1,0:T(8,128)(2,1)}, u32[]{:S(2)}, u32[]{:S(2)}) async-start(bf16[4,256,1024]{2,1,0:T(8,128)(2,1)} %shard_map.69), calls=%async_computation.3 | async-start | bytes 4194304 | tf_op jit(solution)/shard_map/all_to_all | solution.py:242
  127.4 1.0 copy-start.7
  127.4 1.2 copy-start.9
  128.6 3.2 %copy-start.1 = (bf16[1024,512]{1,0:T(8,128)(2,1)S(1)}, bf16[1024,512]{1,0:T(8,128)(2,1)}, u32[]{:S(2)}) copy-start(bf16[1024,512]{1,0:T(8,128)(2,1)} %copy-done) | copy-start | bytes 3145732
  131.9 6.0 %copy-start.5 = (bf16[2,512,512]{2,1,0:T(8,128)(2,1)S(1)}, bf16[2,512,512]{2,1,0:T(8,128)(2,1)}, u32[]{:S(2)}) copy-start(bf16[2,512,512]{2,1,0:T(8,128)(2,1)} %copy-done.4) | copy-start | bytes 3145732
  135.6 1.0 copy-start.2
  137.5 19.3 %copy-start.3 = (bf16[2,512,512]{2,1,0:T(8,128)(2,1)S(1)}, bf16[2,512,512]{2,1,0:T(8,128)(2,1)}, u32[]{:S(2)}) copy-start(bf16[2,512,512]{2,1,0:T(8,128)(2,1)} %copy-done.2) | copy-start | bytes 3145732
  137.5 11.1 %collective-permute-start.9 = (bf16[512,512]{1,0:T(8,128)(2,1)}, bf16[512,512]{1,0:T(8,128)(2,1)}, u32[]{:S(2)}, u32[]{:S(2)}) collective-permute-start(bf16[512,512]{1,0:T(8,128)(2,1)} %dynamic-slice_bitcast_fusion.4), channel_id=1, source_target_pairs={{0,1},{1,0},{4,5},{5,4},{8,9},{9,8},{12,13},{13,12},{16,17},{17,16... | collective-permute-start | bytes 1572872 | tf_op jit(solution)/shard_map/ppermute | solution.py:34
  139.8 17.0 %collective-permute-start.11 = (bf16[512,512]{1,0:T(8,128)(2,1)}, bf16[512,512]{1,0:T(8,128)(2,1)}, u32[]{:S(2)}, u32[]{:S(2)}) collective-permute-start(bf16[512,512]{1,0:T(8,128)(2,1)} %fusion.11), channel_id=1, source_target_pairs={{32,0},{33,1},{36,4},{37,5},{40,8},{41,9},{44,12},{45,13},{48,16},... | collective-permute-start | bytes 1572872 | tf_op jit(solution)/shard_map/ppermute | solution.py:34
  143.0 26.6 %collective-permute-start.15 = (bf16[1024,256]{1,0:T(8,128)(2,1)}, bf16[1024,256]{1,0:T(8,128)(2,1)}, u32[]{:S(2)}, u32[]{:S(2)}) collective-permute-start(bf16[1024,256]{1,0:T(8,128)(2,1)} %get-tuple-element.36), channel_id=1, source_target_pairs={{0,2},{1,3},{4,6},{5,7},{8,10},{9,11},{12,14},{13,15},{16,18},{17,... | collective-permute-start | bytes 1572872 | tf_op jit(solution)/shard_map/ppermute | solution.py:34
  146.5 32.0 %collective-permute-start.14 = (bf16[1024,256]{1,0:T(8,128)(2,1)}, bf16[1024,256]{1,0:T(8,128)(2,1)}, u32[]{:S(2)}, u32[]{:S(2)}) collective-permute-start(bf16[1024,256]{1,0:T(8,128)(2,1)} %get-tuple-element.37), channel_id=1, source_target_pairs={{0,34},{1,35},{4,38},{5,39},{8,42},{9,43},{12,46},{13,47},{16,50},... | collective-permute-start | bytes 1572872 | tf_op jit(solution)/shard_map/ppermute | solution.py:34
  148.4 30.2 %collective-permute-start.13 = (bf16[1024,256]{1,0:T(8,128)(2,1)}, bf16[1024,256]{1,0:T(8,128)(2,1)}, u32[]{:S(2)}, u32[]{:S(2)}) collective-permute-start(bf16[1024,256]{1,0:T(8,128)(2,1)} %get-tuple-element.35), channel_id=1, source_target_pairs={{0,32},{1,33},{4,36},{5,37},{8,40},{9,41},{12,44},{13,45},{16,48},... | collective-permute-start | bytes 1572872 | tf_op jit(solution)/shard_map/ppermute | solution.py:34
  159.0 26.1 %all-to-all-start.2 = ((bf16[8,64,512]{2,1,0:T(8,128)(2,1)}), bf16[8,64,512]{2,1,0:T(8,128)(2,1)S(1)}, u32[]{:S(2)}, u32[]{:S(2)}) async-start(bf16[8,64,512]{2,1,0:T(8,128)(2,1)} %bitcast.92), calls=%async_computation.2 | async-start | bytes 1048576 | tf_op jit(solution)/shard_map/all_to_all | solution.py:242
  180.3 1.4 collective-permute-start.16
  185.1 16.5 %all-to-all-start.4 = ((bf16[8,128,256]{2,1,0:T(8,128)(2,1)}), bf16[8,128,256]{2,1,0:T(8,128)(2,1)S(1)}, u32[]{:S(2)}, u32[]{:S(2)}) async-start(bf16[8,128,256]{2,1,0:T(8,128)(2,1)} %bitcast.21), calls=%async_computation.4 | async-start | bytes 1048576 | tf_op jit(solution)/shard_map/all_to_all | solution.py:242
  191.1 7.9 %collective-permute-start.19 = (bf16[256,256]{1,0:T(8,128)(2,1)S(1)}, bf16[256,256]{1,0:T(8,128)(2,1)S(1)}, u32[]{:S(2)}, u32[]{:S(2)}) collective-permute-start(bf16[256,256]{1,0:T(8,128)(2,1)S(1)} %get-tuple-element.59), channel_id=1, source_target_pairs={{0,128},{1,129},{4,132},{5,133},{8,136},{9,137},{12,140},{13,141},... | collective-permute-start | bytes 393224 | tf_op jit(solution)/shard_map/ppermute | solution.py:34
  193.9 7.5 %collective-permute-start.18 = (bf16[256,256]{1,0:T(8,128)(2,1)S(1)}, bf16[256,256]{1,0:T(8,128)(2,1)S(1)}, u32[]{:S(2)}, u32[]{:S(2)}) collective-permute-start(bf16[256,256]{1,0:T(8,128)(2,1)S(1)} %get-tuple-element.58), channel_id=1, source_target_pairs={{0,192},{1,193},{4,196},{5,197},{8,200},{9,201},{12,204},{13,205},... | collective-permute-start | bytes 393224 | tf_op jit(solution)/shard_map/ppermute | solution.py:34
  193.9 7.5 %collective-permute-start.17 = (bf16[256,256]{1,0:T(8,128)(2,1)S(1)}, bf16[256,256]{1,0:T(8,128)(2,1)S(1)}, u32[]{:S(2)}, u32[]{:S(2)}) collective-permute-start(bf16[256,256]{1,0:T(8,128)(2,1)S(1)} %get-tuple-element.57), channel_id=1, source_target_pairs={{0,64},{1,65},{4,68},{5,69},{8,72},{9,73},{12,76},{13,77},{16,80},... | collective-permute-start | bytes 393224 | tf_op jit(solution)/shard_map/ppermute | solution.py:34
  197.2 9.6 %collective-permute-start.12 = (bf16[4,64,512]{2,1,0:T(8,128)(2,1)S(1)}, bf16[4,64,512]{2,1,0:T(8,128)(2,1)S(1)}, u32[]{:S(2)}, u32[]{:S(2)}) collective-permute-start(bf16[4,64,512]{2,1,0:T(8,128)(2,1)S(1)} %dynamic-slice_bitcast_fusion.5), channel_id=1, source_target_pairs={{0,1},{1,0},{4,5},{5,4},{8,9},{9,8},{12,13},{13,12},{16,17},{17,16... | collective-permute-start | bytes 786440 | tf_op jit(solution)/shard_map/ppermute | solution.py:34
  202.4 16.4 %all-to-all-start.5 = ((bf16[8,4,16,256]{3,2,1,0:T(8,128)(2,1)}), bf16[8,4,16,256]{3,2,1,0:T(8,128)(2,1)S(1)}, u32[]{:S(2)}, u32[]{:S(2)}) async-start(bf16[8,4,16,256]{3,2,1,0:T(8,128)(2,1)} %copy.35), calls=%async_computation.5 | async-start | bytes 524288 | tf_op jit(solution)/shard_map/all_to_all | solution.py:242
where the time goes:
time: 222 us; the launch traced here: 220 us
  waiting for transfers between devices  85.7 us (39%)
  starting transfers between devices  57.2 us (26%)
  Pallas kernels  32.8 us (15%)
  other arithmetic  26 us (12%)
  local copies, waits for them, and re-layouts  11.8 us (5%)
  matrix products  5.59 us (3%)
    ppermute x20, waiting for transfers between devices, move(): return lax.ppermute(value, BOTH, pairs)  64.8 us
    all_to_all x6, starting transfers between devices, regroup(): lax.all_to_all(value, names, 0, 0, axis_index_groups=groups, tiled=True)  34.1 us
    ppermute x20, starting transfers between devices, move(): return lax.ppermute(value, BOTH, pairs)  23.1 us
    all_to_all x6, waiting for transfers between devices, regroup(): lax.all_to_all(value, names, 0, 0, axis_index_groups=groups, tiled=True)  20.8 us
    pallas_call x1, Pallas kernels, attention(): pl.pallas_call(attention_kernel, grid=(pairs,), in_specs=[pl.BlockSpec(me...  17.4 us
    pallas_call x2, Pallas kernels, token_grad(): pl.pallas_call(token_grad_kernel, grid=(1,), in_specs=specs + [tokens, co...  7.17 us
    dot_general x2, matrix products, mm(): lax.dot_general(a, b, (((ca,), (cb,)), ((), ())), preferred_element_type=...  5.59 us
    pallas_call x1, Pallas kernels, weight_grads_a(): pl.pallas_call(weight_grad_a_kernel, grid=(1,), in_specs=[pl.BlockSpec((1...  4.97 us
  transfers between devices with their start and end apart: 26, of which 11 were waited for; matrix products, arithmetic and copies ran while one was open for 13% of the time, Pallas kernels for 5%

commit v1 on v0

--- a/solution.py
+++ b/solution.py
@@ -242,17 +242,25 @@
     return lax.all_to_all(value, names, 0, 0, axis_index_groups=groups, tiled=True)
 
 
-def total(value, parts):
-    return jnp.sum(value.reshape((parts,) + (-1,) + value.shape[1:]).astype(F32), axis=0)
-
-
-def spread_sum(value, here, target):
-    came = []
-    for step in (1, 3, 2):
-        chunk = lax.dynamic_index_in_dim(value, lax.rem(here + step, 4), 0, keepdims=False)
-        came.append(move(chunk, lambda y, x, z, c, step=step: target(step, y, x, z, c)))
-    mine = lax.dynamic_index_in_dim(value, here, 0, keepdims=False)
-    return mine.astype(F32) + came[0].astype(F32) + came[1].astype(F32) + came[2].astype(F32)
+def after(value, *events):
+    return lax.optimization_barrier((value,) + events)[0]
+
+
+def chunks(value, here):
+    return [
+        lax.dynamic_index_in_dim(value, lax.rem(here + step, 4), 0, keepdims=False) for step in (0, 1, 3, 2)
+    ]
+
+
+def spread_sum(pieces, target, *events):
+    out = pieces[0].astype(F32)
+    came = [
+        move(piece, lambda y, x, z, c, step=step: target(step, y, x, z, c))
+        for step, piece in zip((1, 3, 2), pieces[1:])
+    ]
+    for piece in came:
+        out = out + after(piece, *events).astype(F32)
+    return out.astype(BF16)
 
 
 def along_y(step, y, x, z, c):
@@ -265,7 +273,6 @@
 
 ALL_Y, ALL_X, ALL_Z, ALL_C = range(NY), range(NX), range(NZ), range(2)
 Z_GROUPS = [[ring * NZ + z for z in ALL_Z] for ring in range(8)]
-Y_GROUPS = [[(y * 2 + xl) * NZ + z for y in ALL_Y] for xl in range(2) for z in ALL_Z]
 XC_GROUPS = [
     [flat(y, 2 * xh + xl, z, c) for xl in range(2) for xh in range(2) for c in ALL_C] for y in ALL_Y for z in ALL_Z
 ]
@@ -304,14 +311,30 @@
     def across(y, x, z, c):
         return (y, 3 - x, z, c)
 
-    near_give = jnp.concatenate([qkv_weight[:, 256:512], groups_of(out_weight, 1 - core)], axis=0)
-    near = jnp.concatenate(
-        [qkv_weight[:, :256], qkv_weight[:, 512:], groups_of(out_weight, core)], axis=0
-    )
-    far_give = move(near_give, across)
-    far = move(near, across)
-    near_swap = other_core(near_give)
-    far_swap = other_core(far_give)
+    cross = jnp.concatenate(
+        [
+            lax.dynamic_slice_in_dim(qkv_weight, y * 256, 256, 0),
+            lax.dynamic_slice_in_dim(out_weight, y * 256, 256, 0),
+        ],
+        axis=1,
+    )
+    cross = move(cross, across)
+    far_rows = jnp.zeros((1024, 1024), BF16)
+    far_rows = lax.dynamic_update_slice_in_dim(far_rows, cross, y * 256, 0)
+    for step in (1, 3, 2):
+        piece = move(cross, lambda y, x, z, c, step=step: (y + step, x, z, c))
+        far_rows = lax.dynamic_update_slice_in_dim(far_rows, piece, lax.rem(y + 4 - step, 4) * 256, 0)
+
+    def to_give(qkv, out):
+        return jnp.concatenate([qkv[:, 256:512], groups_of(out, 1 - core)], axis=0)
+
+    def to_keep(qkv, out):
+        return jnp.concatenate([qkv[:, :256], qkv[:, 512:768], groups_of(out, core)], axis=0)
+
+    near = to_keep(qkv_weight, out_weight)
+    far = to_keep(far_rows, far_rows[:, 768:])
+    near_swap = other_core(to_give(qkv_weight, out_weight))
+    far_swap = other_core(to_give(far_rows, far_rows[:, 768:]))
 
     def to_chips(tokens):
         low, high = tokens[..., :512], tokens[..., 512:]
@@ -355,20 +378,19 @@
         return mine.astype(F32) + other.astype(F32)
 
     ig_halo = token_grad(0, weight, None, dk, dv)
-    returned = move(core_sum(ig_halo).astype(BF16), last_ring)
-    dq, dk, dv, ig_halo = lax.optimization_barrier((dq, dk, dv, ig_halo))
-
-    part_a = weight_grads_a(src_t, dq, dk, dv)
-    dq, dk, dv, part_a = lax.optimization_barrier((dq, dk, dv, part_a))
-    part_a = total(regroup(part_a, "seq", Y_GROUPS), NY)[0].astype(BF16)
-
-    part_c = weight_grads_c(src_t, dq, dv, att_t, cot)
-    dq, dk, dv, part_c = lax.optimization_barrier((dq, dk, dv, part_c))
-    part_c = spread_sum(part_c, x, along_x).astype(BF16)
-
-    ig = core_sum(token_grad(1, weight, dq, dk, dv))
-    ig = (ig + returned.astype(F32)).astype(BF16).reshape(8, 64, 512)
+
+    part_a = chunks(weight_grads_a(src_t, dq, after(dk, ig_halo), dv), y)
+    ig_halo = core_sum(ig_halo).astype(BF16)
+    returned = move(ig_halo, last_ring)
+
+    part_c = chunks(weight_grads_c(src_t, after(dq, ig_halo, *part_a), dv, att_t, cot), x)
+    ig = token_grad(1, weight, after(dq, *part_c), dk, dv)
+    part_a = spread_sum(part_a, along_y, ig)
+    part_c = spread_sum(part_c, along_x, ig)
+
+    ig = (core_sum(ig) + returned.astype(F32)).astype(BF16).reshape(8, 64, 512)
     ig = regroup(ig, "seq", Z_GROUPS).reshape(2, 4, 64, 512)
+    part_a = after(part_a, ig)
     kept = lax.dynamic_index_in_dim(ig, core, 0, keepdims=False)
     came = other_core(lax.dynamic_index_in_dim(ig, 1 - core, 0, keepdims=False))
     input_grad = in_order(kept, came, -1)[None]
@@ -382,7 +404,7 @@
     other = other_core(lax.dynamic_index_in_dim(part_o, 1 - core, 0, keepdims=False))
     part_o = in_order(mine, other, 1).reshape(4, 128, 256)
     part_c = jnp.concatenate([part_c[:512].reshape(4, 128, 256), part_o], axis=1)
-    part_c = spread_sum(part_c, y, along_y).astype(BF16).reshape(2, 128, 256)
+    part_c = spread_sum(chunks(part_c, y), along_y).reshape(2, 128, 256)
 
     last = jnp.concatenate([part_a, part_c], axis=0).reshape(4, 8, 16, 256).transpose(1, 0, 2, 3)
     last = jnp.sum(regroup(last, "seq", Z_GROUPS).astype(F32), axis=0)

time: 222 us -> 191 us (0.86)
  waiting for transfers between devices: 85.7 us -> 56.7 us
  other arithmetic: 26 us -> 18.8 us
  local copies, waits for them, and re-layouts: 11.8 us -> 17.1 us
  starting transfers between devices: 57.2 us -> 60 us
    ppermute x20 -> x25, waiting for transfers between devices: 64.8 us -> 34.9 us  [move(): return lax.ppermute(value, BOTH, pairs)]
    dynamic_update_slice x0 -> x4, local copies, waits for them, and re-layouts: none -> 4.32 us  [the longest x3 3.24 us: body(): lax.dynamic_update_slice_in_dim(far_rows, piece, lax.rem(y + 4 - step, 4)...]
    unnamed x26 -> x16, local copies, waits for them, and re-layouts: 3.87 us -> 1.14 us
    ppermute x20 -> x25, starting transfers between devices: 23.1 us -> 25.1 us  [move(): return lax.ppermute(value, BOTH, pairs)]
    convert_element_type x4 -> x5, other arithmetic: 5.85 us -> 4.04 us  [the longest x3 2.91 us: spread_sum(): return out.astype(BF16)]
    all_to_all x6 -> x5, waiting for transfers between devices: 20.8 us -> 21.9 us  [regroup(): lax.all_to_all(value, names, 0, 0, axis_index_groups=groups, tiled=True)]
    all_to_all x6 -> x5, starting transfers between devices: 34.1 us -> 34.9 us  [regroup(): lax.all_to_all(value, names, 0, 0, axis_index_groups=groups, tiled=True)]
  transfers between devices with their start and end apart: 26 -> 30, of which waited for: 11 -> 13; matrix products, arithmetic and copies ran while one was open for 13% -> 16% of each run, Pallas kernels for 5% -> 6%
where the time goes in v1:
time: 191 us; the launch traced here: 190 us
  starting transfers between devices  60 us (31%)
  waiting for transfers between devices  56.7 us (30%)
  Pallas kernels  30.8 us (16%)
  other arithmetic  18.8 us (10%)
  local copies, waits for them, and re-layouts  17.1 us (9%)
  matrix products  5.58 us (3%)
    all_to_all x5, starting transfers between devices, regroup(): lax.all_to_all(value, names, 0, 0, axis_index_groups=groups, tiled=True)  34.9 us
    ppermute x25, waiting for transfers between devices, move(): return lax.ppermute(value, BOTH, pairs)  34.9 us
    ppermute x25, starting transfers between devices, move(): return lax.ppermute(value, BOTH, pairs)  25.1 us
    all_to_all x5, waiting for transfers between devices, regroup(): lax.all_to_all(value, names, 0, 0, axis_index_groups=groups, tiled=True)  21.9 us
    pallas_call x1, Pallas kernels, attention(): pl.pallas_call(attention_kernel, grid=(pairs,), in_specs=[pl.BlockSpec(me...  17.5 us
    pallas_call x2, Pallas kernels, token_grad(): pl.pallas_call(token_grad_kernel, grid=(1,), in_specs=specs + [tokens, co...  6.51 us
    dot_general x2, matrix products, mm(): lax.dot_general(a, b, (((ca,), (cb,)), ((), ())), preferred_element_type=...  5.58 us
  transfers between devices with their start and end apart: 30, of which 13 were waited for; matrix products, arithmetic and copies ran while one was open for 16% of the time, Pallas kernels for 6%

profile of v1, /device:TPU:24, one launch (start us, length us, event | category | flops | bytes accessed | tf_op | source)
XLA Modules:
  0.0 190.1 jit_solution(4441094657290698174)
XLA Ops:
  0.7 1.1 constant_dynamic-slice_fusion
  1.8 1.0 constant_dynamic-slice_fusion.1
  2.8 0.9 pad_maximum_fusion.9
  3.7 2.8 %collective-permute-start.3 = (bf16[256,1024]{1,0:T(8,128)(2,1)}, bf16[256,1024]{1,0:T(8,128)(2,1)}, u32[]{:S(2)}, u32[]{:S(2)}) collective-permute-start(bf16[256,1024]{1,0:T(8,128)(2,1)} %pad_maximum_fusion.9), channel_id=1, source_target_pairs={{0,34},{1,35},{4,38},{5,39},{8,42},{9,43},{12,46},{13,47},{16,50},... | collective-permute-start | bytes 1572872 | tf_op jit(solution)/shard_map/ppermute | solution.py:34
  6.6 0.7 broadcast_select_fusion.14
  7.8 1.2 fusion.25
  9.1 0.8 pad_maximum_fusion.8
  9.9 8.5 %all-to-all-start = ((bf16[8,64,512]{2,1,0:T(8,128)(2,1)}), bf16[8,64,512]{2,1,0:T(8,128)(2,1)S(1)}, u32[]{:S(2)}, u32[]{:S(2)}) async-start(bf16[8,64,512]{2,1,0:T(8,128)(2,1)} %pad_maximum_fusion.8), calls=%async_computation | async-start | bytes 1048576 | tf_op jit(solution)/shard_map/all_to_all | solution.py:242
  18.4 0.7 dynamic-slice_bitcast_fusion.19
  19.3 1.0 pad_maximum_fusion.6
  20.3 1.8 collective-permute-start.5
  22.1 1.2 collective-permute-start.6
  23.3 1.0 broadcast_select_fusion.13
  24.3 0.9 pad_maximum_fusion.10
  25.4 1.1 constant_dynamic-update-slice_fusion.3
  26.5 7.7 %collective-permute-done.4 = bf16[256,1024]{1,0:T(8,128)(2,1)} collective-permute-done((bf16[256,1024]{1,0:T(8,128)(2,1)}, bf16[256,1024]{1,0:T(8,128)(2,1)}, u32[]{:S(2)}, u32[]{:S(2)}) %collective-permute-start.4) | collective-permute-done | bytes 524320 | tf_op jit(solution)/shard_map/ppermute | solution.py:34
  34.2 1.1 constant_dynamic-update-slice_fusion.2
  35.3 0.8 all-to-all-done
  36.0 7.6 %all-to-all-start.1 = ((bf16[8,64,512]{2,1,0:T(8,128)(2,1)}), bf16[8,64,512]{2,1,0:T(8,128)(2,1)S(1)}, u32[]{:S(2)}, u32[]{:S(2)}) async-start(bf16[8,64,512]{2,1,0:T(8,128)(2,1)} %pad_maximum_fusion.10), calls=%async_computation.1 | async-start | bytes 1048576 | tf_op jit(solution)/shard_map/all_to_all | solution.py:242
  43.6 3.8 %collective-permute-done.5 = bf16[256,1024]{1,0:T(8,128)(2,1)} collective-permute-done((bf16[256,1024]{1,0:T(8,128)(2,1)}, bf16[256,1024]{1,0:T(8,128)(2,1)}, u32[]{:S(2)}, u32[]{:S(2)}) %collective-permute-start.5) | collective-permute-done | bytes 524320 | tf_op jit(solution)/shard_map/ppermute | solution.py:34
  47.4 1.1 constant_dynamic-update-slice_fusion.1
  48.4 1.1 constant_dynamic-update-slice_fusion
  49.5 1.2 fusion.24
  50.7 0.8 dynamic-slice_bitcast_fusion.17
  51.8 2.1 %collective-permute-start.1 = (bf16[512,512]{0,1:T(8,128)(2,1)S(1)}, bf16[512,512]{0,1:T(8,128)(2,1)S(1)}, u32[]{:S(2)}, u32[]{:S(2)}) collective-permute-start(bf16[512,512]{0,1:T(8,128)(2,1)S(1)} %copy.32), channel_id=1, source_target_pairs={{0,32},{1,33},{4,36},{5,37},{8,40},{9,41},{12,44},{13,45},{16,48},... | collective-permute-start | bytes 1572872 | tf_op jit(solution)/shard_map/ppermute | solution.py:34
  53.9 1.0 pad_maximum_fusion.7
  55.1 2.5 %all-to-all-done.1 = bf16[8,64,512]{2,1,0:T(8,128)(2,1)S(1)} async-done(((bf16[8,64,512]{2,1,0:T(8,128)(2,1)}), bf16[8,64,512]{2,1,0:T(8,128)(2,1)S(1)}, u32[]{:S(2)}, u32[]{:S(2)}) %all-to-all-start.1) | async-done | bytes 524320 | tf_op jit(solution)/shard_map/all_to_all | solution.py:242
  57.6 1.8 broadcast_select_fusion
  59.4 7.5 %collective-permute-done.1 = bf16[512,512]{0,1:T(8,128)(2,1)S(1)} collective-permute-done((bf16[512,512]{0,1:T(8,128)(2,1)S(1)}, bf16[512,512]{0,1:T(8,128)(2,1)S(1)}, u32[]{:S(2)}, u32[]{:S(2)}) %collective-permute-start.1) | collective-permute-done | bytes 524320 | tf_op jit(solution)/shard_map/ppermute | solution.py:34
  67.5 1.5 broadcast_select_fusion.4
  69.3 0.7 convolution_convert_fusion.1.g_ref
  71.2 1.1 copy-done
  72.3 4.8 %convolution_convert_fusion.q_ref.k_ref.v_ref = bf16[1024,1536]{1,0:T(8,128)(2,1)} fusion(bf16[1024,1536]{1,0:T(8,128)(2,1)S(1)} %select_dynamic-update-slice_fusion.refs_1_.refs_3_.refs_5_, bf16[1024,512]{0,1:T(8,128)(2,1)S(1)} %get-tuple-element.46, bf16[1024,512]{0,1:T(8,128)(2,1)S(1)} %get-tuple-element.45), kind=kOutput, calls=%fused_computation | convolution fusion | flops 3226992640 | bytes 8388608 | tf_op jit(solution)/shard_map/dot_general | solution.py:42
  77.2 17.5 %shard_map.67 = (bf16[512,512]{1,0:T(8,128)(2,1)S(1)}, bf16[512,512]{1,0:T(8,128)(2,1)S(1)}, bf16[1024,512]{1,0:T(8,128)(2,1)S(1)}, bf16[1024,512]{1,0:T(8,128)(2,1)S(1)}) custom-call(f32[1,1]{1,0:T(1,128)} %bitcast.bias_ref, bf16[1024,1536]{1,0:T(8,128)(2,1)} %convolution_convert_fusion.q_ref.k_ref.v_ref, ...), custom_call_target="tpu_custom_call" | custom-call | flops 2415919104 | bytes 6291456 | tf_op jit(solution)/shard_map/pallas_call | solution.py:122
  94.7 2.8 %shard_map.68 = bf16[2,512,512]{2,1,0:T(8,128)(2,1)S(1)} custom-call(bf16[1024,512]{1,0:T(8,128)(2,1)S(1)} %get-tuple-element.20.refs_0_.dk_ref.refs_2_, bf16[1024,1536]{1,0:T(8,128)(2,1)} %copy-done, bf16[1024,512]{1,0:T(8,128)(2,1)S(1)} %get-tuple-element.19.refs_2_.dv_ref.refs_4_, bf16[1024,1536]{1,0:T(8,128)(2,1)} %copy-done), custom_call_target="tpu_custom_call" | custom-call | flops 1073741824 | bytes 5242880 | tf_op jit(solution)/shard_map/pallas_call | solution.py:168
  98.2 1.5 fusion.src_ref
  99.8 3.7 %shard_map.69 = bf16[4,256,1024]{2,1,0:T(8,128)(2,1)S(1)} custom-call(bf16[1024,1024]{1,0:T(8,128)(2,1)} %fusion.src_ref, bf16[512,512]{1,0:T(8,128)(2,1)S(1)} %get-tuple-element.23.dq_ref.refs_0_, bf16[1024,512]{1,0:T(8,128)(2,1)S(1)} %get-tuple-element.20.refs_0_.dk_ref.refs_2_, bf16[1024,512]{1,0:T(8,128)(2,1)S(1)} %get-tuple-element.19.refs_2_.dv_ref.refs_4_), custom_call_target="tpu_custom_call" | custom-call | flops 1887436800 | bytes 6291456 | tf_op jit(solution)/shard_map/pallas_call | solution.py:207
  103.4 1.2 dynamic-slice_bitcast_fusion.5
  104.8 4.0 %collective-permute-start.13 = (bf16[512,512]{1,0:T(8,128)(2,1)S(1)}, bf16[512,512]{1,0:T(8,128)(2,1)S(1)}, u32[]{:S(2)}, u32[]{:S(2)}) collective-permute-start(bf16[512,512]{1,0:T(8,128)(2,1)S(1)} %fusion.10), channel_id=1, source_target_pairs={{32,0},{33,1},{36,4},{37,5},{40,8},{41,9},{44,12},{45,13},{48,16},... | collective-permute-start | bytes 1572872 | tf_op jit(solution)/shard_map/ppermute | solution.py:34
  108.8 3.1 %shard_map.70 = bf16[4,1024,256]{2,1,0:T(8,128)(2,1)S(1)} custom-call(bf16[1024,1024]{1,0:T(8,128)(2,1)} %fusion.src_ref, bf16[512,512]{1,0:T(8,128)(2,1)S(1)} %get-tuple-element.23.dq_ref.refs_0_, bf16[1024,512]{1,0:T(8,128)(2,1)S(1)} %get-tuple-element.19.refs_2_.dv_ref.refs_4_, bf16[512,512]{1,0:T(8,128)(2,1)S(1)} %get-tuple-element.22.att_ref, ...), custom_call_target="tpu_custom_call" | custom-call | flops 1342177280 | bytes 6291456 | tf_op jit(solution)/shard_map/pallas_call | solution.py:224
  111.9 1.2 dynamic-slice_bitcast_fusion.1
  113.1 3.7 %shard_map.71 = bf16[2,512,512]{2,1,0:T(8,128)(2,1)S(1)} custom-call(bf16[512,512]{1,0:T(8,128)(2,1)S(1)} %get-tuple-element.23.dq_ref.refs_0_, bf16[1024,1536]{1,0:T(8,128)(2,1)} %copy-done, bf16[1024,512]{1,0:T(8,128)(2,1)S(1)} %get-tuple-element.20.refs_0_.dk_ref.refs_2_, bf16[1024,1536]{1,0:T(8,128)(2,1)} %copy-done, ...), custom_call_target="tpu_custom_call" | custom-call | flops 1610612736 | bytes 5242880 | tf_op jit(solution)/shard_map/pallas_call | solution.py:168
  117.0 4.1 %collective-permute-start.20 = (bf16[1024,256]{1,0:T(8,128)(2,1)}, bf16[1024,256]{1,0:T(8,128)(2,1)S(1)}, u32[]{:S(2)}, u32[]{:S(2)}) collective-permute-start(bf16[1024,256]{1,0:T(8,128)(2,1)} %get-tuple-element.33), channel_id=1, source_target_pairs={{0,2},{1,3},{4,6},{5,7},{8,10},{9,11},{12,14},{13,15},{16,18},{17,... | collective-permute-start | bytes 1572872 | tf_op jit(solution)/shard_map/ppermute | solution.py:34
  121.0 2.0 %collective-permute-start.18 = (bf16[1024,256]{1,0:T(8,128)(2,1)}, bf16[1024,256]{1,0:T(8,128)(2,1)}, u32[]{:S(2)}, u32[]{:S(2)}) collective-permute-start(bf16[1024,256]{1,0:T(8,128)(2,1)} %get-tuple-element.35), channel_id=1, source_target_pairs={{0,32},{1,33},{4,36},{5,37},{8,40},{9,41},{12,44},{13,45},{16,48},... | collective-permute-start | bytes 1572872 | tf_op jit(solution)/shard_map/ppermute | solution.py:34
  123.1 0.6 collective-permute-start.17
  123.7 0.6 collective-permute-start.16
  124.4 1.0 fusion.9
  125.4 7.4 %all-to-all-start.2 = ((bf16[8,64,512]{2,1,0:T(8,128)(2,1)}), bf16[8,64,512]{2,1,0:T(8,128)(2,1)S(1)}, u32[]{:S(2)}, u32[]{:S(2)}) async-start(bf16[8,64,512]{2,1,0:T(8,128)(2,1)} %bitcast.28), calls=%async_computation.2 | async-start | bytes 1048576 | tf_op jit(solution)/shard_map/all_to_all | solution.py:242
  132.8 3.8 %collective-permute-done.20 = bf16[1024,256]{1,0:T(8,128)(2,1)S(1)} collective-permute-done((bf16[1024,256]{1,0:T(8,128)(2,1)}, bf16[1024,256]{1,0:T(8,128)(2,1)S(1)}, u32[]{:S(2)}, u32[]{:S(2)}) %collective-permute-start.20) | collective-permute-done | bytes 524320 | tf_op jit(solution)/shard_map/ppermute | solution.py:34
  136.5 7.8 %collective-permute-done.19 = bf16[1024,256]{1,0:T(8,128)(2,1)} collective-permute-done((bf16[1024,256]{1,0:T(8,128)(2,1)}, bf16[1024,256]{1,0:T(8,128)(2,1)}, u32[]{:S(2)}, u32[]{:S(2)}) %collective-permute-start.19) | collective-permute-done | bytes 524320 | tf_op jit(solution)/shard_map/ppermute | solution.py:34
  144.3 2.6 %collective-permute-done.18 = bf16[1024,256]{1,0:T(8,128)(2,1)} collective-permute-done((bf16[1024,256]{1,0:T(8,128)(2,1)}, bf16[1024,256]{1,0:T(8,128)(2,1)}, u32[]{:S(2)}, u32[]{:S(2)}) %collective-permute-start.18) | collective-permute-done | bytes 524320 | tf_op jit(solution)/shard_map/ppermute | solution.py:34
  146.9 1.5 add_convert_fusion
  148.6 0.7 collective-permute-done.16
  149.2 0.6 collective-permute-done.21
  150.4 1.1 collective-permute-start.23
  151.5 2.2 %collective-permute-start.22 = (bf16[256,256]{1,0:T(8,128)(2,1)S(1)}, bf16[256,256]{1,0:T(8,128)(2,1)}, u32[]{:S(2)}, u32[]{:S(2)}) collective-permute-start(bf16[256,256]{1,0:T(8,128)(2,1)S(1)} %get-tuple-element.64), channel_id=1, source_target_pairs={{0,64},{1,65},{4,68},{5,69},{8,72},{9,73},{12,76},{13,77},{16,80},... | collective-permute-start | bytes 393224 | tf_op jit(solution)/shard_map/ppermute | solution.py:34
  154.4 0.9 copy.34
  155.3 4.2 %all-to-all-start.3 = ((bf16[8,128,256]{2,1,0:T(8,128)(2,1)}), bf16[8,128,256]{2,1,0:T(8,128)(2,1)S(1)}, u32[]{:S(2)}, u32[]{:S(2)}) async-start(bf16[8,128,256]{2,1,0:T(8,128)(2,1)} %bitcast.34), calls=%async_computation.3 | async-start | bytes 1048576 | tf_op jit(solution)/shard_map/all_to_all | solution.py:242
  160.1 1.1 fusion.13
  161.2 8.3 %all-to-all-done.3 = bf16[8,128,256]{2,1,0:T(8,128)(2,1)S(1)} async-done(((bf16[8,128,256]{2,1,0:T(8,128)(2,1)}), bf16[8,128,256]{2,1,0:T(8,128)(2,1)S(1)}, u32[]{:S(2)}, u32[]{:S(2)}) %all-to-all-start.3) | async-done | bytes 524320 | tf_op jit(solution)/shard_map/all_to_all | solution.py:242
  169.7 0.7 copy.35
  170.4 7.2 %all-to-all-start.4 = ((bf16[8,4,16,256]{3,2,1,0:T(8,128)(2,1)}), bf16[8,4,16,256]{3,2,1,0:T(8,128)(2,1)S(1)}, u32[]{:S(2)}, u32[]{:S(2)}) async-start(bf16[8,4,16,256]{3,2,1,0:T(8,128)(2,1)} %copy.35), calls=%async_computation.4 | async-start | bytes 524288 | tf_op jit(solution)/shard_map/all_to_all | solution.py:242
  177.7 0.9 maximum_bitcast_fusion
  178.5 10.3 %all-to-all-done.4 = bf16[8,4,16,256]{3,2,1,0:T(8,128)(2,1)S(1)} async-done(((bf16[8,4,16,256]{3,2,1,0:T(8,128)(2,1)}), bf16[8,4,16,256]{3,2,1,0:T(8,128)(2,1)S(1)}, u32[]{:S(2)}, u32[]{:S(2)}) %all-to-all-start.4) | async-done | bytes 262176 | tf_op jit(solution)/shard_map/all_to_all | solution.py:242
  (79 shorter events, 8.0 us)
Async XLA Ops:
  0.6 7.2 %copy-start.1 = (bf16[1024,768]{1,0:T(8,128)(2,1)S(1)}, bf16[1024,768]{1,0:T(8,128)(2,1)}, u32[]{:S(2)}) copy-start(bf16[1024,768]{1,0:T(8,128)(2,1)} %param.6) | copy-start | bytes 4718596
  0.6 5.8 %copy-start.2 = (bf16[1,4,64,1024]{3,2,1,0:T(8,128)(2,1)S(1)}, bf16[1,4,64,1024]{3,2,1,0:T(8,128)(2,1)}, u32[]{:S(2)}) copy-start(bf16[1,4,64,1024]{3,2,1,0:T(8,128)(2,1)} %param.4) | copy-start | bytes 1572868
  0.7 5.9 %copy-start.3 = (bf16[1,4,64,1024]{3,2,1,0:T(8,128)(2,1)S(1)}, bf16[1,4,64,1024]{3,2,1,0:T(8,128)(2,1)}, u32[]{:S(2)}) copy-start(bf16[1,4,64,1024]{3,2,1,0:T(8,128)(2,1)} %param.5) | copy-start | bytes 1572868
  3.7 15.4 %collective-permute-start.3 = (bf16[256,1024]{1,0:T(8,128)(2,1)}, bf16[256,1024]{1,0:T(8,128)(2,1)}, u32[]{:S(2)}, u32[]{:S(2)}) collective-permute-start(bf16[256,1024]{1,0:T(8,128)(2,1)} %pad_maximum_fusion.9), channel_id=1, source_target_pairs={{0,34},{1,35},{4,38},{5,39},{8,42},{9,43},{12,46},{13,47},{16,50},... | collective-permute-start | bytes 1572872 | tf_op jit(solution)/shard_map/ppermute | solution.py:34
  6.5 2.5 %collective-permute-start = (bf16[4,64,512]{2,1,0:T(8,128)(2,1)S(1)}, bf16[4,64,512]{2,1,0:T(8,128)(2,1)S(1)}, u32[]{:S(2)}, u32[]{:S(2)}) collective-permute-start(bf16[4,64,512]{2,1,0:T(8,128)(2,1)S(1)} %broadcast_select_fusion.18), channel_id=1, source_target_pairs={{0,1},{1,0},{4,5},{5,4},{8,9},{9,8},{12,13},{13,12},{16,17},{17,16... | collective-permute-start | bytes 786440 | tf_op jit(solution)/shard_map/ppermute | solution.py:34
  7.3 16.0 %collective-permute-start.9 = (bf16[4,64,512]{2,1,0:T(8,128)(2,1)}, bf16[4,64,512]{2,1,0:T(8,128)(2,1)}, u32[]{:S(2)}, u32[]{:S(2)}) collective-permute-start(bf16[4,64,512]{2,1,0:T(8,128)(2,1)} %broadcast_select_fusion.14), channel_id=1, source_target_pairs={{0,1},{1,0},{4,5},{5,4},{8,9},{9,8},{12,13},{13,12},{16,17},{17,16... | collective-permute-start | bytes 786440 | tf_op jit(solution)/shard_map/ppermute | solution.py:34
  9.0 9.4 %copy-start.7 = (bf16[1024,256]{1,0:T(8,128)(2,1)S(1)}, bf16[1024,256]{1,0:T(8,128)(2,1)}, u32[]{:S(2)}) copy-start(bf16[1024,256]{1,0:T(8,128)(2,1)} %param.7) | copy-start | bytes 1572868
  9.0 10.3 %copy-start.4 = (bf16[1024,256]{1,0:T(8,128)(2,1)S(1)}, bf16[1024,256]{1,0:T(8,128)(2,1)}, u32[]{:S(2)}) copy-start(bf16[1024,256]{1,0:T(8,128)(2,1)} %get-tuple-element.55) | copy-start | bytes 1572868
  9.9 26.1 %all-to-all-start = ((bf16[8,64,512]{2,1,0:T(8,128)(2,1)}), bf16[8,64,512]{2,1,0:T(8,128)(2,1)S(1)}, u32[]{:S(2)}, u32[]{:S(2)}) async-start(bf16[8,64,512]{2,1,0:T(8,128)(2,1)} %pad_maximum_fusion.8), calls=%async_computation | async-start | bytes 1048576 | tf_op jit(solution)/shard_map/all_to_all | solution.py:242
  19.1 15.1 %collective-permute-start.4 = (bf16[256,1024]{1,0:T(8,128)(2,1)}, bf16[256,1024]{1,0:T(8,128)(2,1)}, u32[]{:S(2)}, u32[]{:S(2)}) collective-permute-start(bf16[256,1024]{1,0:T(8,128)(2,1)} %collective-permute-done.3), channel_id=1, source_target_pairs={{0,64},{1,65},{4,68},{5,69},{8,72},{9,73},{12,76},{13,77},{16,80},... | collective-permute-start | bytes 1572872 | tf_op jit(solution)/shard_map/ppermute | solution.py:34
  20.3 47.2 %collective-permute-start.7 = (bf16[1536,256]{1,0:T(8,128)(2,1)}, bf16[1536,256]{1,0:T(8,128)(2,1)}, u32[]{:S(2)}, u32[]{:S(2)}) collective-permute-start(bf16[1536,256]{1,0:T(8,128)(2,1)} %pad_maximum_fusion.6), channel_id=1, source_target_pairs={{0,1},{1,0},{4,5},{5,4},{8,9},{9,8},{12,13},{13,12},{16,17},{17,16... | collective-permute-start | bytes 2359304 | tf_op jit(solution)/shard_map/ppermute | solution.py:34
  20.3 27.1 %collective-permute-start.5 = (bf16[256,1024]{1,0:T(8,128)(2,1)}, bf16[256,1024]{1,0:T(8,128)(2,1)}, u32[]{:S(2)}, u32[]{:S(2)}) collective-permute-start(bf16[256,1024]{1,0:T(8,128)(2,1)} %collective-permute-done.3), channel_id=1, source_target_pairs={{0,192},{1,193},{4,196},{5,197},{8,200},{9,201},{12,204},{13,205},... | collective-permute-start | bytes 1572872 | tf_op jit(solution)/shard_map/ppermute | solution.py:34
  22.1 26.4 %collective-permute-start.6 = (bf16[256,1024]{1,0:T(8,128)(2,1)}, bf16[256,1024]{1,0:T(8,128)(2,1)}, u32[]{:S(2)}, u32[]{:S(2)}) collective-permute-start(bf16[256,1024]{1,0:T(8,128)(2,1)} %collective-permute-done.3), channel_id=1, source_target_pairs={{0,128},{1,129},{4,132},{5,133},{8,136},{9,137},{12,140},{13,141},... | collective-permute-start | bytes 1572872 | tf_op jit(solution)/shard_map/ppermute | solution.py:34
  36.0 21.5 %all-to-all-start.1 = ((bf16[8,64,512]{2,1,0:T(8,128)(2,1)}), bf16[8,64,512]{2,1,0:T(8,128)(2,1)S(1)}, u32[]{:S(2)}, u32[]{:S(2)}) async-start(bf16[8,64,512]{2,1,0:T(8,128)(2,1)} %pad_maximum_fusion.10), calls=%async_computation.1 | async-start | bytes 1048576 | tf_op jit(solution)/shard_map/all_to_all | solution.py:242
  50.7 3.2 %copy-start.5 = (bf16[1024,256]{1,0:T(8,128)(2,1)S(1)}, bf16[1024,256]{1,0:T(8,128)(2,1)}, u32[]{:S(2)}) copy-start(bf16[1024,256]{1,0:T(8,128)(2,1)} %get-tuple-element.48) | copy-start | bytes 1572868
  50.7 6.8 %copy-start.6 = (bf16[1024,256]{1,0:T(8,128)(2,1)S(1)}, bf16[1024,256]{1,0:T(8,128)(2,1)}, u32[]{:S(2)}) copy-start(bf16[1024,256]{1,0:T(8,128)(2,1)} %get-tuple-element.53) | copy-start | bytes 1572868
  51.8 15.1 %collective-permute-start.1 = (bf16[512,512]{0,1:T(8,128)(2,1)S(1)}, bf16[512,512]{0,1:T(8,128)(2,1)S(1)}, u32[]{:S(2)}, u32[]{:S(2)}) collective-permute-start(bf16[512,512]{0,1:T(8,128)(2,1)S(1)} %copy.32), channel_id=1, source_target_pairs={{0,32},{1,33},{4,36},{5,37},{8,40},{9,41},{12,44},{13,45},{16,48},... | collective-permute-start | bytes 1572872 | tf_op jit(solution)/shard_map/ppermute | solution.py:34
  55.0 12.5 %collective-permute-start.8 = (bf16[1536,256]{1,0:T(8,128)(2,1)S(1)}, bf16[1536,256]{1,0:T(8,128)(2,1)}, u32[]{:S(2)}, u32[]{:S(2)}) collective-permute-start(bf16[1536,256]{1,0:T(8,128)(2,1)S(1)} %pad_maximum_fusion.7), channel_id=1, source_target_pairs={{0,1},{1,0},{4,5},{5,4},{8,9},{9,8},{12,13},{13,12},{16,17},{17,16... | collective-permute-start | bytes 2359304 | tf_op jit(solution)/shard_map/ppermute | solution.py:34
  57.6 9.8 %collective-permute-start.10 = (bf16[512,512]{1,0:T(8,128)(2,1)S(1)}, bf16[512,512]{1,0:T(8,128)(2,1)S(1)}, u32[]{:S(2)}, u32[]{:S(2)}) collective-permute-start(bf16[512,512]{1,0:T(8,128)(2,1)S(1)} %bitcast.107), channel_id=1, source_target_pairs={{0,1},{1,0},{4,5},{5,4},{8,9},{9,8},{12,13},{13,12},{16,17},{17,16... | collective-permute-start | bytes 1572872 | tf_op jit(solution)/shard_map/ppermute | solution.py:34
  67.0 3.7 %collective-permute-start.2 = (bf16[1024,512]{0,1:T(8,128)(2,1)S(1)}, bf16[1024,512]{0,1:T(8,128)(2,1)S(1)}, u32[]{:S(2)}, u32[]{:S(2)}) collective-permute-start(bf16[1024,512]{0,1:T(8,128)(2,1)S(1)} %pad_maximum_fusion.4), channel_id=1, source_target_pairs={{0,1},{1,0},{4,5},{5,4},{8,9},{9,8},{12,13},{13,12},{16,17},{17,16... | collective-permute-start | bytes 3145736 | tf_op jit(solution)/shard_map/ppermute | solution.py:34
  70.7 1.6 copy-start
  97.5 7.1 %collective-permute-start.11 = (bf16[512,512]{1,0:T(8,128)(2,1)S(1)}, bf16[512,512]{1,0:T(8,128)(2,1)S(1)}, u32[]{:S(2)}, u32[]{:S(2)}) collective-permute-start(bf16[512,512]{1,0:T(8,128)(2,1)S(1)} %dynamic-slice_bitcast_fusion.9), channel_id=1, source_target_pairs={{0,1},{1,0},{4,5},{5,4},{8,9},{9,8},{12,13},{13,12},{16,17},{17,16... | collective-permute-start | bytes 1572872 | tf_op jit(solution)/shard_map/ppermute | solution.py:34
  104.8 18.3 %collective-permute-start.13 = (bf16[512,512]{1,0:T(8,128)(2,1)S(1)}, bf16[512,512]{1,0:T(8,128)(2,1)S(1)}, u32[]{:S(2)}, u32[]{:S(2)}) collective-permute-start(bf16[512,512]{1,0:T(8,128)(2,1)S(1)} %fusion.10), channel_id=1, source_target_pairs={{32,0},{33,1},{36,4},{37,5},{40,8},{41,9},{44,12},{45,13},{48,16},... | collective-permute-start | bytes 1572872 | tf_op jit(solution)/shard_map/ppermute | solution.py:34
  116.9 6.9 %collective-permute-start.12 = (bf16[512,512]{1,0:T(8,128)(2,1)S(1)}, bf16[512,512]{1,0:T(8,128)(2,1)S(1)}, u32[]{:S(2)}, u32[]{:S(2)}) collective-permute-start(bf16[512,512]{1,0:T(8,128)(2,1)S(1)} %dynamic-slice_bitcast_fusion), channel_id=1, source_target_pairs={{0,1},{1,0},{4,5},{5,4},{8,9},{9,8},{12,13},{13,12},{16,17},{17,16... | collective-permute-start | bytes 1572872 | tf_op jit(solution)/shard_map/ppermute | solution.py:34
  117.0 19.6 %collective-permute-start.20 = (bf16[1024,256]{1,0:T(8,128)(2,1)}, bf16[1024,256]{1,0:T(8,128)(2,1)S(1)}, u32[]{:S(2)}, u32[]{:S(2)}) collective-permute-start(bf16[1024,256]{1,0:T(8,128)(2,1)} %get-tuple-element.33), channel_id=1, source_target_pairs={{0,2},{1,3},{4,6},{5,7},{8,10},{9,11},{12,14},{13,15},{16,18},{17,... | collective-permute-start | bytes 1572872 | tf_op jit(solution)/shard_map/ppermute | solution.py:34
  121.0 23.3 %collective-permute-start.19 = (bf16[1024,256]{1,0:T(8,128)(2,1)}, bf16[1024,256]{1,0:T(8,128)(2,1)}, u32[]{:S(2)}, u32[]{:S(2)}) collective-permute-start(bf16[1024,256]{1,0:T(8,128)(2,1)} %get-tuple-element.34), channel_id=1, source_target_pairs={{0,34},{1,35},{4,38},{5,39},{8,42},{9,43},{12,46},{13,47},{16,50},... | collective-permute-start | bytes 1572872 | tf_op jit(solution)/shard_map/ppermute | solution.py:34
  121.0 25.9 %collective-permute-start.18 = (bf16[1024,256]{1,0:T(8,128)(2,1)}, bf16[1024,256]{1,0:T(8,128)(2,1)}, u32[]{:S(2)}, u32[]{:S(2)}) collective-permute-start(bf16[1024,256]{1,0:T(8,128)(2,1)} %get-tuple-element.35), channel_id=1, source_target_pairs={{0,32},{1,33},{4,36},{5,37},{8,40},{9,41},{12,44},{13,45},{16,48},... | collective-permute-start | bytes 1572872 | tf_op jit(solution)/shard_map/ppermute | solution.py:34
  123.1 25.5 %collective-permute-start.17 = (bf16[256,1024]{1,0:T(8,128)(2,1)}, bf16[256,1024]{1,0:T(8,128)(2,1)S(1)}, u32[]{:S(2)}, u32[]{:S(2)}) collective-permute-start(bf16[256,1024]{1,0:T(8,128)(2,1)} %get-tuple-element.37), channel_id=1, source_target_pairs={{0,128},{1,129},{4,132},{5,133},{8,136},{9,137},{12,140},{13,141},... | collective-permute-start | bytes 1572872 | tf_op jit(solution)/shard_map/ppermute | solution.py:34
  123.7 25.5 %collective-permute-start.16 = (bf16[256,1024]{1,0:T(8,128)(2,1)}, bf16[256,1024]{1,0:T(8,128)(2,1)S(1)}, u32[]{:S(2)}, u32[]{:S(2)}) collective-permute-start(bf16[256,1024]{1,0:T(8,128)(2,1)} %get-tuple-element.38), channel_id=1, source_target_pairs={{0,192},{1,193},{4,196},{5,197},{8,200},{9,201},{12,204},{13,205},... | collective-permute-start | bytes 1572872 | tf_op jit(solution)/shard_map/ppermute | solution.py:34
  125.4 28.6 %all-to-all-start.2 = ((bf16[8,64,512]{2,1,0:T(8,128)(2,1)}), bf16[8,64,512]{2,1,0:T(8,128)(2,1)S(1)}, u32[]{:S(2)}, u32[]{:S(2)}) async-start(bf16[8,64,512]{2,1,0:T(8,128)(2,1)} %bitcast.28), calls=%async_computation.2 | async-start | bytes 1048576 | tf_op jit(solution)/shard_map/all_to_all | solution.py:242
  136.5 12.7 %collective-permute-start.15 = (bf16[256,1024]{1,0:T(8,128)(2,1)}, bf16[256,1024]{1,0:T(8,128)(2,1)S(1)}, u32[]{:S(2)}, u32[]{:S(2)}) collective-permute-start(bf16[256,1024]{1,0:T(8,128)(2,1)} %get-tuple-element.39), channel_id=1, source_target_pairs={{0,64},{1,65},{4,68},{5,69},{8,72},{9,73},{12,76},{13,77},{16,80},... | collective-permute-start | bytes 1572872 | tf_op jit(solution)/shard_map/ppermute | solution.py:34
  148.5 1.4 collective-permute-start.21
  150.0 9.5 %collective-permute-start.24 = (bf16[256,256]{1,0:T(8,128)(2,1)S(1)}, bf16[256,256]{1,0:T(8,128)(2,1)}, u32[]{:S(2)}, u32[]{:S(2)}) collective-permute-start(bf16[256,256]{1,0:T(8,128)(2,1)S(1)} %get-tuple-element.66), channel_id=1, source_target_pairs={{0,128},{1,129},{4,132},{5,133},{8,136},{9,137},{12,140},{13,141},... | collective-permute-start | bytes 393224 | tf_op jit(solution)/shard_map/ppermute | solution.py:34
  150.4 9.5 %collective-permute-start.23 = (bf16[256,256]{1,0:T(8,128)(2,1)S(1)}, bf16[256,256]{1,0:T(8,128)(2,1)}, u32[]{:S(2)}, u32[]{:S(2)}) collective-permute-start(bf16[256,256]{1,0:T(8,128)(2,1)S(1)} %get-tuple-element.65), channel_id=1, source_target_pairs={{0,192},{1,193},{4,196},{5,197},{8,200},{9,201},{12,204},{13,205},... | collective-permute-start | bytes 393224 | tf_op jit(solution)/shard_map/ppermute | solution.py:34
  151.5 8.4 %collective-permute-start.22 = (bf16[256,256]{1,0:T(8,128)(2,1)S(1)}, bf16[256,256]{1,0:T(8,128)(2,1)}, u32[]{:S(2)}, u32[]{:S(2)}) collective-permute-start(bf16[256,256]{1,0:T(8,128)(2,1)S(1)} %get-tuple-element.64), channel_id=1, source_target_pairs={{0,64},{1,65},{4,68},{5,69},{8,72},{9,73},{12,76},{13,77},{16,80},... | collective-permute-start | bytes 393224 | tf_op jit(solution)/shard_map/ppermute | solution.py:34
  155.3 14.3 %all-to-all-start.3 = ((bf16[8,128,256]{2,1,0:T(8,128)(2,1)}), bf16[8,128,256]{2,1,0:T(8,128)(2,1)S(1)}, u32[]{:S(2)}, u32[]{:S(2)}) async-start(bf16[8,128,256]{2,1,0:T(8,128)(2,1)} %bitcast.34), calls=%async_computation.3 | async-start | bytes 1048576 | tf_op jit(solution)/shard_map/all_to_all | solution.py:242
  159.9 17.7 %collective-permute-start.14 = (bf16[4,64,512]{2,1,0:T(8,128)(2,1)S(1)}, bf16[4,64,512]{2,1,0:T(8,128)(2,1)S(1)}, u32[]{:S(2)}, u32[]{:S(2)}) collective-permute-start(bf16[4,64,512]{2,1,0:T(8,128)(2,1)S(1)} %dynamic-slice_bitcast_fusion.10), channel_id=1, source_target_pairs={{0,1},{1,0},{4,5},{5,4},{8,9},{9,8},{12,13},{13,12},{16,17},{17,16... | collective-permute-start | bytes 786440 | tf_op jit(solution)/shard_map/ppermute | solution.py:34
  170.4 18.5 %all-to-all-start.4 = ((bf16[8,4,16,256]{3,2,1,0:T(8,128)(2,1)}), bf16[8,4,16,256]{3,2,1,0:T(8,128)(2,1)S(1)}, u32[]{:S(2)}, u32[]{:S(2)}) async-start(bf16[8,4,16,256]{3,2,1,0:T(8,128)(2,1)} %copy.35), calls=%async_computation.4 | async-start | bytes 524288 | tf_op jit(solution)/shard_map/all_to_all | solution.py:242

commit v2 on v1

--- a/solution.py
+++ b/solution.py
@@ -49,6 +49,7 @@
     upper = (
         lax.broadcasted_iota(jnp.int32, (size, size), 0) > lax.broadcasted_iota(jnp.int32, (size, size), 1)
     )
+    upper_low = jnp.where(upper, 1.0, 0.0).astype(BF16)
     factor = LOG2E * HD ** -0.5
     tiles = [slice(i * size, (i + 1) * size) for i in range(4)]
     keys = [k_ref[tile, :] for tile in tiles]
@@ -84,9 +85,10 @@
             scale = 1.0 / (jnp.sum(edge, axis=0, keepdims=True) + jnp.sum(full, axis=0, keepdims=True))
             edge = edge * scale
             full = full * scale
-            p0 = jnp.where(upper, edge, 0.0).astype(BF16)
+            edge_low = edge.astype(BF16)
+            p0 = edge_low * upper_low
             p1 = full.astype(BF16)
-            p2 = jnp.where(upper, 0.0, edge).astype(BF16)
+            p2 = edge_low - p0
             att = (
                 mm(vals_t[block][lanes], p0, 1, 0)
                 + mm(vals_t[block + 1][lanes], p1, 1, 0)
@@ -95,10 +97,10 @@
             delta = jnp.sum(g_t[lanes] * att, axis=0, keepdims=True)
             att_ref[lanes, rows] = att.astype(BF16)
             d0, d1, d2 = [mm(vals[block + i], g, 1, 1) for i in range(3)]
-            d_edge = edge * (jnp.where(upper, d0, d2) - delta)
-            z0 = jnp.where(upper, d_edge, 0.0).astype(BF16)
+            d_edge = (edge * (jnp.where(upper, d0, d2) - delta)).astype(BF16)
+            z0 = d_edge * upper_low
             z1 = (full * (d1 - delta)).astype(BF16)
-            z2 = jnp.where(upper, 0.0, d_edge).astype(BF16)
+            z2 = d_edge - z0
             dq_t.append(
                 mm(keys_t[block][lanes], z0, 1, 0)
                 + mm(keys_t[block + 1][lanes], z1, 1, 0)
@@ -370,7 +372,7 @@
     qkv = mm(src, weight, 1, 0).astype(BF16)
     g = mm(cot, weight_o, 1, 1).astype(BF16)
     bias = jnp.where(ring == 0, -jnp.inf, 0.0).astype(F32).reshape(1, 1)
-    dq, att_t, dk, dv = attention(bias, qkv, g)
+    dq, att_t, dk, dv = attention(after(bias, src_t), qkv, g)
 
     def core_sum(value):
         mine = lax.dynamic_index_in_dim(value, core, 0, keepdims=False)

time: 191 us -> 205 us (1.073)
  waiting for transfers between devices: 56.7 us -> 65.3 us
  other arithmetic: 18.8 us -> 22 us
    ppermute x25, waiting for transfers between devices: 34.9 us -> 43.1 us  [move(): return lax.ppermute(value, BOTH, pairs)]
  transfers between devices with their start and end apart: 30 -> 30, of which waited for: 13 -> 12; matrix products, arithmetic and copies ran while one was open for 16% -> 15% of each run, Pallas kernels for 6% -> 2%
where the time goes in v2:
time: 205 us; the launch traced here: 202 us
  waiting for transfers between devices  65.3 us (32%)
  starting transfers between devices  58.9 us (29%)
  Pallas kernels  31.1 us (15%)
  other arithmetic  22 us (11%)
  local copies, waits for them, and re-layouts  18 us (9%)
  matrix products  5.61 us (3%)
    ppermute x25, waiting for transfers between devices, move(): return lax.ppermute(value, BOTH, pairs)  43.1 us
    all_to_all x5, starting transfers between devices, regroup(): lax.all_to_all(value, names, 0, 0, axis_index_groups=groups, tiled=True)  33.3 us
    ppermute x25, starting transfers between devices, move(): return lax.ppermute(value, BOTH, pairs)  25.6 us
    all_to_all x5, waiting for transfers between devices, regroup(): lax.all_to_all(value, names, 0, 0, axis_index_groups=groups, tiled=True)  22.3 us
    pallas_call x1, Pallas kernels, attention(): pl.pallas_call(attention_kernel, grid=(pairs,), in_specs=[pl.BlockSpec(me...  17.4 us
    pallas_call x2, Pallas kernels, token_grad(): pl.pallas_call(token_grad_kernel, grid=(1,), in_specs=specs + [tokens, co...  6.89 us
    dot_general x2, matrix products, mm(): lax.dot_general(a, b, (((ca,), (cb,)), ((), ())), preferred_element_type=...  5.61 us
  transfers between devices with their start and end apart: 30, of which 12 were waited for; matrix products, arithmetic and copies ran while one was open for 15% of the time, Pallas kernels for 2%

profile of v2, /device:TPU:24, one launch (start us, length us, event | category | flops | bytes accessed | tf_op | source)
XLA Modules:
  0.0 202.1 jit_solution(2842633621378111072)
XLA Ops:
  0.7 1.2 constant_dynamic-slice_fusion.1
  1.9 0.9 constant_dynamic-slice_fusion
  2.8 0.9 pad_maximum_fusion.9
  3.7 2.8 %collective-permute-start.3 = (bf16[256,1024]{1,0:T(8,128)(2,1)}, bf16[256,1024]{1,0:T(8,128)(2,1)}, u32[]{:S(2)}, u32[]{:S(2)}) collective-permute-start(bf16[256,1024]{1,0:T(8,128)(2,1)} %pad_maximum_fusion.9), channel_id=1, source_target_pairs={{0,34},{1,35},{4,38},{5,39},{8,42},{9,43},{12,46},{13,47},{16,50},... | collective-permute-start | bytes 1572872 | tf_op jit(solution)/shard_map/ppermute | solution.py:34
  6.4 0.8 broadcast_select_fusion.14
  7.2 0.7 broadcast_select_fusion.18
  8.4 1.1 fusion.25
  9.9 0.8 pad_maximum_fusion.8
  10.7 8.5 %all-to-all-start = ((bf16[8,64,512]{2,1,0:T(8,128)(2,1)}), bf16[8,64,512]{2,1,0:T(8,128)(2,1)S(1)}, u32[]{:S(2)}, u32[]{:S(2)}) async-start(bf16[8,64,512]{2,1,0:T(8,128)(2,1)} %pad_maximum_fusion.8), calls=%async_computation | async-start | bytes 1048576 | tf_op jit(solution)/shard_map/all_to_all | solution.py:244
  19.5 0.9 pad_maximum_fusion.6
  20.5 1.8 collective-permute-start.5
  22.3 1.2 collective-permute-start.6
  23.5 1.0 broadcast_select_fusion.13
  24.5 0.8 pad_maximum_fusion.10
  25.7 1.1 constant_dynamic-update-slice_fusion.3
  26.7 7.7 %collective-permute-done.4 = bf16[256,1024]{1,0:T(8,128)(2,1)} collective-permute-done((bf16[256,1024]{1,0:T(8,128)(2,1)}, bf16[256,1024]{1,0:T(8,128)(2,1)}, u32[]{:S(2)}, u32[]{:S(2)}) %collective-permute-start.4) | collective-permute-done | bytes 524320 | tf_op jit(solution)/shard_map/ppermute | solution.py:34
  34.4 1.1 constant_dynamic-update-slice_fusion.2
  35.5 1.7 all-to-all-done
  37.2 0.8 copy-done.10
  38.0 6.4 %all-to-all-start.1 = ((bf16[8,64,512]{2,1,0:T(8,128)(2,1)}), bf16[8,64,512]{2,1,0:T(8,128)(2,1)S(1)}, u32[]{:S(2)}, u32[]{:S(2)}) async-start(bf16[8,64,512]{2,1,0:T(8,128)(2,1)} %pad_maximum_fusion.10), calls=%async_computation.1 | async-start | bytes 1048576 | tf_op jit(solution)/shard_map/all_to_all | solution.py:244
  44.4 3.2 %collective-permute-done.5 = bf16[256,1024]{1,0:T(8,128)(2,1)} collective-permute-done((bf16[256,1024]{1,0:T(8,128)(2,1)}, bf16[256,1024]{1,0:T(8,128)(2,1)}, u32[]{:S(2)}, u32[]{:S(2)}) %collective-permute-start.5) | collective-permute-done | bytes 524320 | tf_op jit(solution)/shard_map/ppermute | solution.py:34
  47.6 1.1 constant_dynamic-update-slice_fusion.1
  48.7 1.1 constant_dynamic-update-slice_fusion
  49.8 1.2 fusion.24
  51.0 0.8 dynamic-slice_bitcast_fusion.17
  51.8 1.3 copy.32
  53.0 2.1 %collective-permute-start.1 = (bf16[512,512]{0,1:T(8,128)(2,1)S(1)}, bf16[512,512]{0,1:T(8,128)(2,1)S(1)}, u32[]{:S(2)}, u32[]{:S(2)}) collective-permute-start(bf16[512,512]{0,1:T(8,128)(2,1)S(1)} %copy.32), channel_id=1, source_target_pairs={{0,32},{1,33},{4,36},{5,37},{8,40},{9,41},{12,44},{13,45},{16,48},... | collective-permute-start | bytes 1572872 | tf_op jit(solution)/shard_map/ppermute | solution.py:34
  55.2 1.9 pad_maximum_fusion.7
  57.1 2.3 %all-to-all-done.1 = bf16[8,64,512]{2,1,0:T(8,128)(2,1)S(1)} async-done(((bf16[8,64,512]{2,1,0:T(8,128)(2,1)}), bf16[8,64,512]{2,1,0:T(8,128)(2,1)S(1)}, u32[]{:S(2)}, u32[]{:S(2)}) %all-to-all-start.1) | async-done | bytes 524320 | tf_op jit(solution)/shard_map/all_to_all | solution.py:244
  59.4 1.6 broadcast_select_fusion
  61.0 7.5 %collective-permute-done.1 = bf16[512,512]{0,1:T(8,128)(2,1)S(1)} collective-permute-done((bf16[512,512]{0,1:T(8,128)(2,1)S(1)}, bf16[512,512]{0,1:T(8,128)(2,1)S(1)}, u32[]{:S(2)}, u32[]{:S(2)}) %collective-permute-start.1) | collective-permute-done | bytes 524320 | tf_op jit(solution)/shard_map/ppermute | solution.py:34
  69.1 1.8 broadcast_select_fusion.4
  71.3 0.7 convolution_convert_fusion.1.g_ref
  73.2 1.8 fusion.src_ref
  75.1 4.9 %convolution_convert_fusion.q_ref.k_ref.v_ref = bf16[1024,1536]{1,0:T(8,128)(2,1)} fusion(bf16[1024,1536]{1,0:T(8,128)(2,1)S(1)} %select_dynamic-update-slice_fusion.refs_1_.refs_3_.refs_5_, bf16[1024,512]{0,1:T(8,128)(2,1)S(1)} %get-tuple-element.52, bf16[1024,512]{0,1:T(8,128)(2,1)S(1)} %get-tuple-element.51), kind=kOutput, calls=%fused_computation | convolution fusion | flops 3226992640 | bytes 8388608 | tf_op jit(solution)/shard_map/dot_general | solution.py:42
  79.9 17.4 %shard_map.67 = (bf16[512,512]{1,0:T(8,128)(2,1)S(1)}, bf16[512,512]{1,0:T(8,128)(2,1)S(1)}, bf16[1024,512]{1,0:T(8,128)(2,1)S(1)}, bf16[1024,512]{1,0:T(8,128)(2,1)S(1)}) custom-call(f32[1,1]{1,0:T(1,128)} %bitcast.bias_ref, bf16[1024,1536]{1,0:T(8,128)(2,1)} %convolution_convert_fusion.q_ref.k_ref.v_ref, ...), custom_call_target="tpu_custom_call" | custom-call | flops 2415919104 | bytes 6291456 | tf_op jit(solution)/shard_map/pallas_call | solution.py:124
  97.4 3.2 %shard_map.68 = bf16[2,512,512]{2,1,0:T(8,128)(2,1)S(1)} custom-call(bf16[1024,512]{1,0:T(8,128)(2,1)S(1)} %get-tuple-element.22.refs_0_.dk_ref.refs_2_, bf16[1024,1536]{1,0:T(8,128)(2,1)} %copy-done.4, bf16[1024,512]{1,0:T(8,128)(2,1)S(1)} %get-tuple-element.21.refs_2_.dv_ref.refs_4_, bf16[1024,1536]{1,0:T(8,128)(2,1)} %copy-done.4), custom_call_target="tpu_custom_call" | custom-call | flops 1073741824 | bytes 5242880 | tf_op jit(solution)/shard_map/pallas_call | solution.py:170
  100.6 0.8 dynamic-slice_bitcast_fusion.9
  101.9 1.4 pad_maximum_fusion.5.cot_ref
  103.3 3.7 %shard_map.69 = bf16[4,256,1024]{2,1,0:T(8,128)(2,1)S(1)} custom-call(bf16[1024,1024]{1,0:T(8,128)(2,1)} %fusion.src_ref, bf16[512,512]{1,0:T(8,128)(2,1)S(1)} %copy-done.1, bf16[1024,512]{1,0:T(8,128)(2,1)S(1)} %get-tuple-element.22.refs_0_.dk_ref.refs_2_, bf16[1024,512]{1,0:T(8,128)(2,1)S(1)} %get-tuple-element.21.refs_2_.dv_ref.refs_4_), custom_call_target="tpu_custom_call" | custom-call | flops 1887436800 | bytes 6291456 | tf_op jit(solution)/shard_map/pallas_call | solution.py:209
  107.0 1.4 dynamic-slice_bitcast_fusion.5
  108.4 1.2 fusion.10
  109.6 3.1 %shard_map.70 = bf16[4,1024,256]{2,1,0:T(8,128)(2,1)S(1)} custom-call(bf16[1024,1024]{1,0:T(8,128)(2,1)} %fusion.src_ref, bf16[512,512]{1,0:T(8,128)(2,1)S(1)} %copy-done.1, bf16[1024,512]{1,0:T(8,128)(2,1)S(1)} %get-tuple-element.21.refs_2_.dv_ref.refs_4_, bf16[512,512]{1,0:T(8,128)(2,1)S(1)} %copy-done.3, bf16[512,1024]{1,0:T(8,128)(2,1)S(1)} %pad_maximum_fusion.5.cot_ref), custom_call_target="tpu_custom_call" | custom-call | flops 1342177280 | bytes 6291456 | tf_op jit(solution)/shard_map/pallas_call | solution.py:226
  112.7 1.2 dynamic-slice_bitcast_fusion.1
  113.9 3.7 %shard_map.71 = bf16[2,512,512]{2,1,0:T(8,128)(2,1)S(1)} custom-call(bf16[512,512]{1,0:T(8,128)(2,1)S(1)} %copy-done.1, bf16[1024,1536]{1,0:T(8,128)(2,1)} %copy-done.4, bf16[1024,512]{1,0:T(8,128)(2,1)S(1)} %get-tuple-element.22.refs_0_.dk_ref.refs_2_, bf16[1024,1536]{1,0:T(8,128)(2,1)} %copy-done.4, ...), custom_call_target="tpu_custom_call" | custom-call | flops 1610612736 | bytes 5242880 | tf_op jit(solution)/shard_map/pallas_call | solution.py:170
  117.8 3.9 %collective-permute-start.13 = (bf16[512,512]{1,0:T(8,128)(2,1)S(1)}, bf16[512,512]{1,0:T(8,128)(2,1)S(1)}, u32[]{:S(2)}, u32[]{:S(2)}) collective-permute-start(bf16[512,512]{1,0:T(8,128)(2,1)S(1)} %fusion.10), channel_id=1, source_target_pairs={{32,0},{33,1},{36,4},{37,5},{40,8},{41,9},{44,12},{45,13},{48,16},... | collective-permute-start | bytes 1572872 | tf_op jit(solution)/shard_map/ppermute | solution.py:34
  121.8 3.2 %collective-permute-start.19 = (bf16[1024,256]{1,0:T(8,128)(2,1)}, bf16[1024,256]{1,0:T(8,128)(2,1)S(1)}, u32[]{:S(2)}, u32[]{:S(2)}) collective-permute-start(bf16[1024,256]{1,0:T(8,128)(2,1)} %get-tuple-element.36), channel_id=1, source_target_pairs={{0,34},{1,35},{4,38},{5,39},{8,42},{9,43},{12,46},{13,47},{16,50},... | collective-permute-start | bytes 1572872 | tf_op jit(solution)/shard_map/ppermute | solution.py:34
  125.0 2.7 %collective-permute-start.20 = (bf16[1024,256]{1,0:T(8,128)(2,1)}, bf16[1024,256]{1,0:T(8,128)(2,1)}, u32[]{:S(2)}, u32[]{:S(2)}) collective-permute-start(bf16[1024,256]{1,0:T(8,128)(2,1)} %get-tuple-element.35), channel_id=1, source_target_pairs={{0,2},{1,3},{4,6},{5,7},{8,10},{9,11},{12,14},{13,15},{16,18},{17,... | collective-permute-start | bytes 1572872 | tf_op jit(solution)/shard_map/ppermute | solution.py:34
  127.7 6.6 %collective-permute-done.13 = bf16[512,512]{1,0:T(8,128)(2,1)S(1)} collective-permute-done((bf16[512,512]{1,0:T(8,128)(2,1)S(1)}, bf16[512,512]{1,0:T(8,128)(2,1)S(1)}, u32[]{:S(2)}, u32[]{:S(2)}) %collective-permute-start.13) | collective-permute-done | bytes 524320 | tf_op jit(solution)/shard_map/ppermute | solution.py:34
  134.4 3.2 %collective-permute-start.16 = (bf16[256,1024]{1,0:T(8,128)(2,1)}, bf16[256,1024]{1,0:T(8,128)(2,1)S(1)}, u32[]{:S(2)}, u32[]{:S(2)}) collective-permute-start(bf16[256,1024]{1,0:T(8,128)(2,1)} %get-tuple-element.40), channel_id=1, source_target_pairs={{0,192},{1,193},{4,196},{5,197},{8,200},{9,201},{12,204},{13,205},... | collective-permute-start | bytes 1572872 | tf_op jit(solution)/shard_map/ppermute | solution.py:34
  137.6 1.0 fusion.9
  138.6 7.2 %all-to-all-start.2 = ((bf16[8,64,512]{2,1,0:T(8,128)(2,1)}), bf16[8,64,512]{2,1,0:T(8,128)(2,1)S(1)}, u32[]{:S(2)}, u32[]{:S(2)}) async-start(bf16[8,64,512]{2,1,0:T(8,128)(2,1)} %bitcast.28), calls=%async_computation.2 | async-start | bytes 1048576 | tf_op jit(solution)/shard_map/all_to_all | solution.py:244
  145.9 14.5 %collective-permute-done.20 = bf16[1024,256]{1,0:T(8,128)(2,1)} collective-permute-done((bf16[1024,256]{1,0:T(8,128)(2,1)}, bf16[1024,256]{1,0:T(8,128)(2,1)}, u32[]{:S(2)}, u32[]{:S(2)}) %collective-permute-start.20) | collective-permute-done | bytes 524320 | tf_op jit(solution)/shard_map/ppermute | solution.py:34
  160.4 1.3 add_convert_fusion
  162.0 1.3 collective-permute-done.21
  163.5 2.0 collective-permute-start.23
  166.6 0.9 copy.34
  167.5 4.0 %all-to-all-start.3 = ((bf16[8,128,256]{2,1,0:T(8,128)(2,1)}), bf16[8,128,256]{2,1,0:T(8,128)(2,1)S(1)}, u32[]{:S(2)}, u32[]{:S(2)}) async-start(bf16[8,128,256]{2,1,0:T(8,128)(2,1)} %bitcast.34), calls=%async_computation.3 | async-start | bytes 1048576 | tf_op jit(solution)/shard_map/all_to_all | solution.py:244
  171.5 1.9 collective-permute-done.23
  173.6 8.0 %all-to-all-done.3 = bf16[8,128,256]{2,1,0:T(8,128)(2,1)S(1)} async-done(((bf16[8,128,256]{2,1,0:T(8,128)(2,1)}), bf16[8,128,256]{2,1,0:T(8,128)(2,1)S(1)}, u32[]{:S(2)}, u32[]{:S(2)}) %all-to-all-start.3) | async-done | bytes 524320 | tf_op jit(solution)/shard_map/all_to_all | solution.py:244
  181.7 0.7 copy.35
  182.4 7.2 %all-to-all-start.4 = ((bf16[8,4,16,256]{3,2,1,0:T(8,128)(2,1)}), bf16[8,4,16,256]{3,2,1,0:T(8,128)(2,1)S(1)}, u32[]{:S(2)}, u32[]{:S(2)}) async-start(bf16[8,4,16,256]{3,2,1,0:T(8,128)(2,1)} %copy.35), calls=%async_computation.4 | async-start | bytes 524288 | tf_op jit(solution)/shard_map/all_to_all | solution.py:244
  189.7 0.9 maximum_bitcast_fusion
  190.5 10.3 %all-to-all-done.4 = bf16[8,4,16,256]{3,2,1,0:T(8,128)(2,1)S(1)} async-done(((bf16[8,4,16,256]{3,2,1,0:T(8,128)(2,1)}), bf16[8,4,16,256]{3,2,1,0:T(8,128)(2,1)S(1)}, u32[]{:S(2)}, u32[]{:S(2)}) %all-to-all-start.4) | async-done | bytes 262176 | tf_op jit(solution)/shard_map/all_to_all | solution.py:244
  (95 shorter events, 7.5 us)
Async XLA Ops:
  0.6 7.8 %copy-start.5 = (bf16[1024,768]{1,0:T(8,128)(2,1)S(1)}, bf16[1024,768]{1,0:T(8,128)(2,1)}, u32[]{:S(2)}) copy-start(bf16[1024,768]{1,0:T(8,128)(2,1)} %param.6) | copy-start | bytes 4718596
  0.6 5.8 %copy-start.7 = (bf16[1,4,64,1024]{3,2,1,0:T(8,128)(2,1)S(1)}, bf16[1,4,64,1024]{3,2,1,0:T(8,128)(2,1)}, u32[]{:S(2)}) copy-start(bf16[1,4,64,1024]{3,2,1,0:T(8,128)(2,1)} %param.5) | copy-start | bytes 1572868
  0.7 6.5 %copy-start.6 = (bf16[1,4,64,1024]{3,2,1,0:T(8,128)(2,1)S(1)}, bf16[1,4,64,1024]{3,2,1,0:T(8,128)(2,1)}, u32[]{:S(2)}) copy-start(bf16[1,4,64,1024]{3,2,1,0:T(8,128)(2,1)} %param.4) | copy-start | bytes 1572868
  3.7 15.6 %collective-permute-start.3 = (bf16[256,1024]{1,0:T(8,128)(2,1)}, bf16[256,1024]{1,0:T(8,128)(2,1)}, u32[]{:S(2)}, u32[]{:S(2)}) collective-permute-start(bf16[256,1024]{1,0:T(8,128)(2,1)} %pad_maximum_fusion.9), channel_id=1, source_target_pairs={{0,34},{1,35},{4,38},{5,39},{8,42},{9,43},{12,46},{13,47},{16,50},... | collective-permute-start | bytes 1572872 | tf_op jit(solution)/shard_map/ppermute | solution.py:34
  7.2 16.4 %collective-permute-start.9 = (bf16[4,64,512]{2,1,0:T(8,128)(2,1)}, bf16[4,64,512]{2,1,0:T(8,128)(2,1)}, u32[]{:S(2)}, u32[]{:S(2)}) collective-permute-start(bf16[4,64,512]{2,1,0:T(8,128)(2,1)} %broadcast_select_fusion.14), channel_id=1, source_target_pairs={{0,1},{1,0},{4,5},{5,4},{8,9},{9,8},{12,13},{13,12},{16,17},{17,16... | collective-permute-start | bytes 786440 | tf_op jit(solution)/shard_map/ppermute | solution.py:34
  7.9 1.9 collective-permute-start
  9.5 9.7 %copy-start.15 = (bf16[1024,256]{1,0:T(8,128)(2,1)S(1)}, bf16[1024,256]{1,0:T(8,128)(2,1)}, u32[]{:S(2)}) copy-start(bf16[1024,256]{1,0:T(8,128)(2,1)} %param.7) | copy-start | bytes 1572868
  10.7 26.5 %all-to-all-start = ((bf16[8,64,512]{2,1,0:T(8,128)(2,1)}), bf16[8,64,512]{2,1,0:T(8,128)(2,1)S(1)}, u32[]{:S(2)}, u32[]{:S(2)}) async-start(bf16[8,64,512]{2,1,0:T(8,128)(2,1)} %pad_maximum_fusion.8), calls=%async_computation | async-start | bytes 1048576 | tf_op jit(solution)/shard_map/all_to_all | solution.py:244
  19.2 15.2 %collective-permute-start.4 = (bf16[256,1024]{1,0:T(8,128)(2,1)}, bf16[256,1024]{1,0:T(8,128)(2,1)}, u32[]{:S(2)}, u32[]{:S(2)}) collective-permute-start(bf16[256,1024]{1,0:T(8,128)(2,1)} %collective-permute-done.3), channel_id=1, source_target_pairs={{0,64},{1,65},{4,68},{5,69},{8,72},{9,73},{12,76},{13,77},{16,80},... | collective-permute-start | bytes 1572872 | tf_op jit(solution)/shard_map/ppermute | solution.py:34
  20.5 48.6 %collective-permute-start.7 = (bf16[1536,256]{1,0:T(8,128)(2,1)}, bf16[1536,256]{1,0:T(8,128)(2,1)}, u32[]{:S(2)}, u32[]{:S(2)}) collective-permute-start(bf16[1536,256]{1,0:T(8,128)(2,1)} %pad_maximum_fusion.6), channel_id=1, source_target_pairs={{0,1},{1,0},{4,5},{5,4},{8,9},{9,8},{12,13},{13,12},{16,17},{17,16... | collective-permute-start | bytes 2359304 | tf_op jit(solution)/shard_map/ppermute | solution.py:34
  20.5 27.1 %collective-permute-start.5 = (bf16[256,1024]{1,0:T(8,128)(2,1)}, bf16[256,1024]{1,0:T(8,128)(2,1)}, u32[]{:S(2)}, u32[]{:S(2)}) collective-permute-start(bf16[256,1024]{1,0:T(8,128)(2,1)} %collective-permute-done.3), channel_id=1, source_target_pairs={{0,192},{1,193},{4,196},{5,197},{8,200},{9,201},{12,204},{13,205},... | collective-permute-start | bytes 1572872 | tf_op jit(solution)/shard_map/ppermute | solution.py:34
  22.3 26.4 %collective-permute-start.6 = (bf16[256,1024]{1,0:T(8,128)(2,1)}, bf16[256,1024]{1,0:T(8,128)(2,1)}, u32[]{:S(2)}, u32[]{:S(2)}) collective-permute-start(bf16[256,1024]{1,0:T(8,128)(2,1)} %collective-permute-done.3), channel_id=1, source_target_pairs={{0,128},{1,129},{4,132},{5,133},{8,136},{9,137},{12,140},{13,141},... | collective-permute-start | bytes 1572872 | tf_op jit(solution)/shard_map/ppermute | solution.py:34
  37.2 0.8 copy-start.10
  38.0 21.4 %all-to-all-start.1 = ((bf16[8,64,512]{2,1,0:T(8,128)(2,1)}), bf16[8,64,512]{2,1,0:T(8,128)(2,1)S(1)}, u32[]{:S(2)}, u32[]{:S(2)}) async-start(bf16[8,64,512]{2,1,0:T(8,128)(2,1)} %pad_maximum_fusion.10), calls=%async_computation.1 | async-start | bytes 1048576 | tf_op jit(solution)/shard_map/all_to_all | solution.py:244
  51.0 4.2 %copy-start.12 = (bf16[1024,256]{1,0:T(8,128)(2,1)S(1)}, bf16[1024,256]{1,0:T(8,128)(2,1)}, u32[]{:S(2)}) copy-start(bf16[1024,256]{1,0:T(8,128)(2,1)} %get-tuple-element.48) | copy-start | bytes 1572868
  51.0 8.4 %copy-start.13 = (bf16[1024,256]{1,0:T(8,128)(2,1)S(1)}, bf16[1024,256]{1,0:T(8,128)(2,1)}, u32[]{:S(2)}) copy-start(bf16[1024,256]{1,0:T(8,128)(2,1)} %get-tuple-element.55) | copy-start | bytes 1572868
  51.0 8.4 %copy-start.14 = (bf16[1024,256]{1,0:T(8,128)(2,1)S(1)}, bf16[1024,256]{1,0:T(8,128)(2,1)}, u32[]{:S(2)}) copy-start(bf16[1024,256]{1,0:T(8,128)(2,1)} %get-tuple-element.56) | copy-start | bytes 1572868
  53.0 15.5 %collective-permute-start.1 = (bf16[512,512]{0,1:T(8,128)(2,1)S(1)}, bf16[512,512]{0,1:T(8,128)(2,1)S(1)}, u32[]{:S(2)}, u32[]{:S(2)}) collective-permute-start(bf16[512,512]{0,1:T(8,128)(2,1)S(1)} %copy.32), channel_id=1, source_target_pairs={{0,32},{1,33},{4,36},{5,37},{8,40},{9,41},{12,44},{13,45},{16,48},... | collective-permute-start | bytes 1572872 | tf_op jit(solution)/shard_map/ppermute | solution.py:34
  57.1 12.0 %collective-permute-start.8 = (bf16[1536,256]{1,0:T(8,128)(2,1)}, bf16[1536,256]{1,0:T(8,128)(2,1)}, u32[]{:S(2)}, u32[]{:S(2)}) collective-permute-start(bf16[1536,256]{1,0:T(8,128)(2,1)} %pad_maximum_fusion.7), channel_id=1, source_target_pairs={{0,1},{1,0},{4,5},{5,4},{8,9},{9,8},{12,13},{13,12},{16,17},{17,16... | collective-permute-start | bytes 2359304 | tf_op jit(solution)/shard_map/ppermute | solution.py:34
  59.4 9.6 %collective-permute-start.10 = (bf16[512,512]{1,0:T(8,128)(2,1)S(1)}, bf16[512,512]{1,0:T(8,128)(2,1)S(1)}, u32[]{:S(2)}, u32[]{:S(2)}) collective-permute-start(bf16[512,512]{1,0:T(8,128)(2,1)S(1)} %bitcast.107), channel_id=1, source_target_pairs={{0,1},{1,0},{4,5},{5,4},{8,9},{9,8},{12,13},{13,12},{16,17},{17,16... | collective-permute-start | bytes 1572872 | tf_op jit(solution)/shard_map/ppermute | solution.py:34
  68.6 4.1 %collective-permute-start.2 = (bf16[1024,512]{0,1:T(8,128)(2,1)S(1)}, bf16[1024,512]{0,1:T(8,128)(2,1)S(1)}, u32[]{:S(2)}, u32[]{:S(2)}) collective-permute-start(bf16[1024,512]{0,1:T(8,128)(2,1)S(1)} %pad_maximum_fusion.4), channel_id=1, source_target_pairs={{0,1},{1,0},{4,5},{5,4},{8,9},{9,8},{12,13},{13,12},{16,17},{17,16... | collective-permute-start | bytes 3145736 | tf_op jit(solution)/shard_map/ppermute | solution.py:34
  69.0 2.3 %copy-start.8 = (bf16[512,512]{1,0:T(8,128)(2,1)}, bf16[512,512]{1,0:T(8,128)(2,1)S(1)}, u32[]{:S(2)}) copy-start(bf16[512,512]{1,0:T(8,128)(2,1)S(1)} %get-tuple-element.58) | copy-start | bytes 1572868
  69.1 2.3 %copy-start.9 = (bf16[512,512]{1,0:T(8,128)(2,1)}, bf16[512,512]{1,0:T(8,128)(2,1)S(1)}, u32[]{:S(2)}) copy-start(bf16[512,512]{1,0:T(8,128)(2,1)S(1)} %get-tuple-element.59) | copy-start | bytes 1572868
  72.7 2.3 %copy-start.4 = (bf16[1024,1536]{1,0:T(8,128)(2,1)}, bf16[1024,1536]{1,0:T(8,128)(2,1)S(1)}, u32[]{:S(2)}) copy-start(bf16[1024,1536]{1,0:T(8,128)(2,1)S(1)} %select_dynamic-update-slice_fusion.refs_1_.refs_3_.refs_5_) | copy-start | bytes 9437188
  97.4 3.2 %copy-start = (bf16[512,512]{1,0:T(8,128)(2,1)}, bf16[512,512]{1,0:T(8,128)(2,1)S(1)}, u32[]{:S(2)}) copy-start(bf16[512,512]{1,0:T(8,128)(2,1)S(1)} %get-tuple-element.25.dq_ref.refs_0_) | copy-start | bytes 1572868
  97.4 3.2 %copy-start.2 = (bf16[512,512]{1,0:T(8,128)(2,1)}, bf16[512,512]{1,0:T(8,128)(2,1)S(1)}, u32[]{:S(2)}) copy-start(bf16[512,512]{1,0:T(8,128)(2,1)S(1)} %get-tuple-element.24.att_ref) | copy-start | bytes 1572868
  101.5 6.9 %collective-permute-start.11 = (bf16[512,512]{1,0:T(8,128)(2,1)}, bf16[512,512]{1,0:T(8,128)(2,1)}, u32[]{:S(2)}, u32[]{:S(2)}) collective-permute-start(bf16[512,512]{1,0:T(8,128)(2,1)} %dynamic-slice_bitcast_fusion.9), channel_id=1, source_target_pairs={{0,1},{1,0},{4,5},{5,4},{8,9},{9,8},{12,13},{13,12},{16,17},{17,16... | collective-permute-start | bytes 1572872 | tf_op jit(solution)/shard_map/ppermute | solution.py:34
  101.9 1.4 copy-start.1
  107.0 2.6 %copy-start.3 = (bf16[512,512]{1,0:T(8,128)(2,1)S(1)}, bf16[512,512]{1,0:T(8,128)(2,1)}, u32[]{:S(2)}) copy-start(bf16[512,512]{1,0:T(8,128)(2,1)} %copy-done.2) | copy-start | bytes 1572868
  117.6 10.1 %collective-permute-start.12 = (bf16[512,512]{1,0:T(8,128)(2,1)S(1)}, bf16[512,512]{1,0:T(8,128)(2,1)S(1)}, u32[]{:S(2)}, u32[]{:S(2)}) collective-permute-start(bf16[512,512]{1,0:T(8,128)(2,1)S(1)} %dynamic-slice_bitcast_fusion), channel_id=1, source_target_pairs={{0,1},{1,0},{4,5},{5,4},{8,9},{9,8},{12,13},{13,12},{16,17},{17,16... | collective-permute-start | bytes 1572872 | tf_op jit(solution)/shard_map/ppermute | solution.py:34
  117.8 16.6 %collective-permute-start.13 = (bf16[512,512]{1,0:T(8,128)(2,1)S(1)}, bf16[512,512]{1,0:T(8,128)(2,1)S(1)}, u32[]{:S(2)}, u32[]{:S(2)}) collective-permute-start(bf16[512,512]{1,0:T(8,128)(2,1)S(1)} %fusion.10), channel_id=1, source_target_pairs={{32,0},{33,1},{36,4},{37,5},{40,8},{41,9},{44,12},{45,13},{48,16},... | collective-permute-start | bytes 1572872 | tf_op jit(solution)/shard_map/ppermute | solution.py:34
  121.7 24.1 %collective-permute-start.18 = (bf16[1024,256]{1,0:T(8,128)(2,1)}, bf16[1024,256]{1,0:T(8,128)(2,1)S(1)}, u32[]{:S(2)}, u32[]{:S(2)}) collective-permute-start(bf16[1024,256]{1,0:T(8,128)(2,1)} %get-tuple-element.37), channel_id=1, source_target_pairs={{0,32},{1,33},{4,36},{5,37},{8,40},{9,41},{12,44},{13,45},{16,48},... | collective-permute-start | bytes 1572872 | tf_op jit(solution)/shard_map/ppermute | solution.py:34
  121.8 24.1 %collective-permute-start.19 = (bf16[1024,256]{1,0:T(8,128)(2,1)}, bf16[1024,256]{1,0:T(8,128)(2,1)S(1)}, u32[]{:S(2)}, u32[]{:S(2)}) collective-permute-start(bf16[1024,256]{1,0:T(8,128)(2,1)} %get-tuple-element.36), channel_id=1, source_target_pairs={{0,34},{1,35},{4,38},{5,39},{8,42},{9,43},{12,46},{13,47},{16,50},... | collective-permute-start | bytes 1572872 | tf_op jit(solution)/shard_map/ppermute | solution.py:34
  125.0 35.5 %collective-permute-start.20 = (bf16[1024,256]{1,0:T(8,128)(2,1)}, bf16[1024,256]{1,0:T(8,128)(2,1)}, u32[]{:S(2)}, u32[]{:S(2)}) collective-permute-start(bf16[1024,256]{1,0:T(8,128)(2,1)} %get-tuple-element.35), channel_id=1, source_target_pairs={{0,2},{1,3},{4,6},{5,7},{8,10},{9,11},{12,14},{13,15},{16,18},{17,... | collective-permute-start | bytes 1572872 | tf_op jit(solution)/shard_map/ppermute | solution.py:34
  127.7 34.2 %collective-permute-start.15 = (bf16[256,1024]{1,0:T(8,128)(2,1)}, bf16[256,1024]{1,0:T(8,128)(2,1)S(1)}, u32[]{:S(2)}, u32[]{:S(2)}) collective-permute-start(bf16[256,1024]{1,0:T(8,128)(2,1)} %get-tuple-element.41), channel_id=1, source_target_pairs={{0,64},{1,65},{4,68},{5,69},{8,72},{9,73},{12,76},{13,77},{16,80},... | collective-permute-start | bytes 1572872 | tf_op jit(solution)/shard_map/ppermute | solution.py:34
  134.4 27.6 %collective-permute-start.16 = (bf16[256,1024]{1,0:T(8,128)(2,1)}, bf16[256,1024]{1,0:T(8,128)(2,1)S(1)}, u32[]{:S(2)}, u32[]{:S(2)}) collective-permute-start(bf16[256,1024]{1,0:T(8,128)(2,1)} %get-tuple-element.40), channel_id=1, source_target_pairs={{0,192},{1,193},{4,196},{5,197},{8,200},{9,201},{12,204},{13,205},... | collective-permute-start | bytes 1572872 | tf_op jit(solution)/shard_map/ppermute | solution.py:34
  138.6 27.7 %all-to-all-start.2 = ((bf16[8,64,512]{2,1,0:T(8,128)(2,1)}), bf16[8,64,512]{2,1,0:T(8,128)(2,1)S(1)}, u32[]{:S(2)}, u32[]{:S(2)}) async-start(bf16[8,64,512]{2,1,0:T(8,128)(2,1)} %bitcast.28), calls=%async_computation.2 | async-start | bytes 1048576 | tf_op jit(solution)/shard_map/all_to_all | solution.py:244
  145.8 16.2 %collective-permute-start.17 = (bf16[256,1024]{1,0:T(8,128)(2,1)}, bf16[256,1024]{1,0:T(8,128)(2,1)S(1)}, u32[]{:S(2)}, u32[]{:S(2)}) collective-permute-start(bf16[256,1024]{1,0:T(8,128)(2,1)} %get-tuple-element.39), channel_id=1, source_target_pairs={{0,128},{1,129},{4,132},{5,133},{8,136},{9,137},{12,140},{13,141},... | collective-permute-start | bytes 1572872 | tf_op jit(solution)/shard_map/ppermute | solution.py:34
  161.7 4.1 %copy-start.11 = (bf16[256,1024]{1,0:T(8,128)(2,1)S(1)}, bf16[256,1024]{1,0:T(8,128)(2,1)}, u32[]{:S(2)}) copy-start(bf16[256,1024]{1,0:T(8,128)(2,1)} %get-tuple-element.42) | copy-start | bytes 1572868
  161.8 1.4 collective-permute-start.21
  163.4 8.1 %collective-permute-start.22 = (bf16[256,256]{1,0:T(8,128)(2,1)S(1)}, bf16[256,256]{1,0:T(8,128)(2,1)S(1)}, u32[]{:S(2)}, u32[]{:S(2)}) collective-permute-start(bf16[256,256]{1,0:T(8,128)(2,1)S(1)} %get-tuple-element.66), channel_id=1, source_target_pairs={{0,64},{1,65},{4,68},{5,69},{8,72},{9,73},{12,76},{13,77},{16,80},... | collective-permute-start | bytes 393224 | tf_op jit(solution)/shard_map/ppermute | solution.py:34
  163.5 9.9 %collective-permute-start.23 = (bf16[256,256]{1,0:T(8,128)(2,1)S(1)}, bf16[256,256]{1,0:T(8,128)(2,1)S(1)}, u32[]{:S(2)}, u32[]{:S(2)}) collective-permute-start(bf16[256,256]{1,0:T(8,128)(2,1)S(1)} %get-tuple-element.67), channel_id=1, source_target_pairs={{0,192},{1,193},{4,196},{5,197},{8,200},{9,201},{12,204},{13,205},... | collective-permute-start | bytes 393224 | tf_op jit(solution)/shard_map/ppermute | solution.py:34
  165.5 7.9 %collective-permute-start.24 = (bf16[256,256]{1,0:T(8,128)(2,1)S(1)}, bf16[256,256]{1,0:T(8,128)(2,1)S(1)}, u32[]{:S(2)}, u32[]{:S(2)}) collective-permute-start(bf16[256,256]{1,0:T(8,128)(2,1)S(1)} %get-tuple-element.68), channel_id=1, source_target_pairs={{0,128},{1,129},{4,132},{5,133},{8,136},{9,137},{12,140},{13,141},... | collective-permute-start | bytes 393224 | tf_op jit(solution)/shard_map/ppermute | solution.py:34
  167.5 14.0 %all-to-all-start.3 = ((bf16[8,128,256]{2,1,0:T(8,128)(2,1)}), bf16[8,128,256]{2,1,0:T(8,128)(2,1)S(1)}, u32[]{:S(2)}, u32[]{:S(2)}) async-start(bf16[8,128,256]{2,1,0:T(8,128)(2,1)} %bitcast.34), calls=%async_computation.3 | async-start | bytes 1048576 | tf_op jit(solution)/shard_map/all_to_all | solution.py:244
  173.4 16.2 %collective-permute-start.14 = (bf16[4,64,512]{2,1,0:T(8,128)(2,1)S(1)}, bf16[4,64,512]{2,1,0:T(8,128)(2,1)S(1)}, u32[]{:S(2)}, u32[]{:S(2)}) collective-permute-start(bf16[4,64,512]{2,1,0:T(8,128)(2,1)S(1)} %dynamic-slice_bitcast_fusion.10), channel_id=1, source_target_pairs={{0,1},{1,0},{4,5},{5,4},{8,9},{9,8},{12,13},{13,12},{16,17},{17,16... | collective-permute-start | bytes 786440 | tf_op jit(solution)/shard_map/ppermute | solution.py:34
  182.4 18.5 %all-to-all-start.4 = ((bf16[8,4,16,256]{3,2,1,0:T(8,128)(2,1)}), bf16[8,4,16,256]{3,2,1,0:T(8,128)(2,1)S(1)}, u32[]{:S(2)}, u32[]{:S(2)}) async-start(bf16[8,4,16,256]{3,2,1,0:T(8,128)(2,1)} %copy.35), calls=%async_computation.4 | async-start | bytes 524288 | tf_op jit(solution)/shard_map/all_to_all | solution.py:244

commit v3 on v2

--- a/solution.py
+++ b/solution.py
@@ -372,7 +372,7 @@
     qkv = mm(src, weight, 1, 0).astype(BF16)
     g = mm(cot, weight_o, 1, 1).astype(BF16)
     bias = jnp.where(ring == 0, -jnp.inf, 0.0).astype(F32).reshape(1, 1)
-    dq, att_t, dk, dv = attention(after(bias, src_t), qkv, g)
+    dq, att_t, dk, dv = attention(bias, qkv, g)
 
     def core_sum(value):
         mine = lax.dynamic_index_in_dim(value, core, 0, keepdims=False)

time: 205 us -> 191 us (0.932)
  waiting for transfers between devices: 65.3 us -> 56.6 us
  other arithmetic: 22 us -> 18.8 us
    ppermute x25, waiting for transfers between devices: 43.1 us -> 34.8 us  [move(): return lax.ppermute(value, BOTH, pairs)]
  transfers between devices with their start and end apart: 30 -> 30, of which waited for: 12 -> 13; matrix products, arithmetic and copies ran while one was open for 15% -> 16% of each run, Pallas kernels for 2% -> 6%
where the time goes in v3:
time: 191 us; the launch traced here: 190 us
  starting transfers between devices  60.1 us (31%)
  waiting for transfers between devices  56.6 us (30%)
  Pallas kernels  30.7 us (16%)
  other arithmetic  18.8 us (10%)
  local copies, waits for them, and re-layouts  17.1 us (9%)
  matrix products  5.58 us (3%)
    all_to_all x5, starting transfers between devices, regroup(): lax.all_to_all(value, names, 0, 0, axis_index_groups=groups, tiled=True)  35 us
    ppermute x25, waiting for transfers between devices, move(): return lax.ppermute(value, BOTH, pairs)  34.8 us
    ppermute x25, starting transfers between devices, move(): return lax.ppermute(value, BOTH, pairs)  25.2 us
    all_to_all x5, waiting for transfers between devices, regroup(): lax.all_to_all(value, names, 0, 0, axis_index_groups=groups, tiled=True)  21.9 us
    pallas_call x1, Pallas kernels, attention(): pl.pallas_call(attention_kernel, grid=(pairs,), in_specs=[pl.BlockSpec(me...  17.4 us
    pallas_call x2, Pallas kernels, token_grad(): pl.pallas_call(token_grad_kernel, grid=(1,), in_specs=specs + [tokens, co...  6.51 us
    dot_general x2, matrix products, mm(): lax.dot_general(a, b, (((ca,), (cb,)), ((), ())), preferred_element_type=...  5.58 us
  transfers between devices with their start and end apart: 30, of which 13 were waited for; matrix products, arithmetic and copies ran while one was open for 16% of the time, Pallas kernels for 6%

profile of v3, /device:TPU:24, one launch (start us, length us, event | category | flops | bytes accessed | tf_op | source)
XLA Modules:
  0.0 190.1 jit_solution(7344988535480205021)
XLA Ops:
  0.7 1.1 constant_dynamic-slice_fusion
  1.8 1.0 constant_dynamic-slice_fusion.1
  2.8 0.9 pad_maximum_fusion.9
  3.7 2.8 %collective-permute-start.3 = (bf16[256,1024]{1,0:T(8,128)(2,1)}, bf16[256,1024]{1,0:T(8,128)(2,1)}, u32[]{:S(2)}, u32[]{:S(2)}) collective-permute-start(bf16[256,1024]{1,0:T(8,128)(2,1)} %pad_maximum_fusion.9), channel_id=1, source_target_pairs={{0,34},{1,35},{4,38},{5,39},{8,42},{9,43},{12,46},{13,47},{16,50},... | collective-permute-start | bytes 1572872 | tf_op jit(solution)/shard_map/ppermute | solution.py:34
  6.6 0.7 broadcast_select_fusion.14
  7.8 1.2 fusion.25
  9.1 0.8 pad_maximum_fusion.8
  9.9 8.5 %all-to-all-start = ((bf16[8,64,512]{2,1,0:T(8,128)(2,1)}), bf16[8,64,512]{2,1,0:T(8,128)(2,1)S(1)}, u32[]{:S(2)}, u32[]{:S(2)}) async-start(bf16[8,64,512]{2,1,0:T(8,128)(2,1)} %pad_maximum_fusion.8), calls=%async_computation | async-start | bytes 1048576 | tf_op jit(solution)/shard_map/all_to_all | solution.py:244
  18.4 0.7 dynamic-slice_bitcast_fusion.19
  19.3 1.0 pad_maximum_fusion.6
  20.3 1.8 collective-permute-start.5
  22.1 1.2 collective-permute-start.6
  23.3 1.0 broadcast_select_fusion.13
  24.3 0.9 pad_maximum_fusion.10
  25.4 1.1 constant_dynamic-update-slice_fusion.3
  26.5 7.7 %collective-permute-done.4 = bf16[256,1024]{1,0:T(8,128)(2,1)} collective-permute-done((bf16[256,1024]{1,0:T(8,128)(2,1)}, bf16[256,1024]{1,0:T(8,128)(2,1)}, u32[]{:S(2)}, u32[]{:S(2)}) %collective-permute-start.4) | collective-permute-done | bytes 524320 | tf_op jit(solution)/shard_map/ppermute | solution.py:34
  34.2 1.1 constant_dynamic-update-slice_fusion.2
  35.3 0.8 all-to-all-done
  36.0 7.6 %all-to-all-start.1 = ((bf16[8,64,512]{2,1,0:T(8,128)(2,1)}), bf16[8,64,512]{2,1,0:T(8,128)(2,1)S(1)}, u32[]{:S(2)}, u32[]{:S(2)}) async-start(bf16[8,64,512]{2,1,0:T(8,128)(2,1)} %pad_maximum_fusion.10), calls=%async_computation.1 | async-start | bytes 1048576 | tf_op jit(solution)/shard_map/all_to_all | solution.py:244
  43.6 3.8 %collective-permute-done.5 = bf16[256,1024]{1,0:T(8,128)(2,1)} collective-permute-done((bf16[256,1024]{1,0:T(8,128)(2,1)}, bf16[256,1024]{1,0:T(8,128)(2,1)}, u32[]{:S(2)}, u32[]{:S(2)}) %collective-permute-start.5) | collective-permute-done | bytes 524320 | tf_op jit(solution)/shard_map/ppermute | solution.py:34
  47.4 1.1 constant_dynamic-update-slice_fusion.1
  48.4 1.1 constant_dynamic-update-slice_fusion
  49.5 1.2 fusion.24
  50.7 0.8 dynamic-slice_bitcast_fusion.17
  51.8 2.1 %collective-permute-start.1 = (bf16[512,512]{0,1:T(8,128)(2,1)S(1)}, bf16[512,512]{0,1:T(8,128)(2,1)S(1)}, u32[]{:S(2)}, u32[]{:S(2)}) collective-permute-start(bf16[512,512]{0,1:T(8,128)(2,1)S(1)} %copy.32), channel_id=1, source_target_pairs={{0,32},{1,33},{4,36},{5,37},{8,40},{9,41},{12,44},{13,45},{16,48},... | collective-permute-start | bytes 1572872 | tf_op jit(solution)/shard_map/ppermute | solution.py:34
  53.9 1.0 pad_maximum_fusion.7
  55.1 2.5 %all-to-all-done.1 = bf16[8,64,512]{2,1,0:T(8,128)(2,1)S(1)} async-done(((bf16[8,64,512]{2,1,0:T(8,128)(2,1)}), bf16[8,64,512]{2,1,0:T(8,128)(2,1)S(1)}, u32[]{:S(2)}, u32[]{:S(2)}) %all-to-all-start.1) | async-done | bytes 524320 | tf_op jit(solution)/shard_map/all_to_all | solution.py:244
  57.6 1.8 broadcast_select_fusion
  59.4 7.5 %collective-permute-done.1 = bf16[512,512]{0,1:T(8,128)(2,1)S(1)} collective-permute-done((bf16[512,512]{0,1:T(8,128)(2,1)S(1)}, bf16[512,512]{0,1:T(8,128)(2,1)S(1)}, u32[]{:S(2)}, u32[]{:S(2)}) %collective-permute-start.1) | collective-permute-done | bytes 524320 | tf_op jit(solution)/shard_map/ppermute | solution.py:34
  67.5 1.5 broadcast_select_fusion.4
  69.3 0.7 convolution_convert_fusion.1.g_ref
  71.2 1.1 copy-done
  72.3 4.8 %convolution_convert_fusion.q_ref.k_ref.v_ref = bf16[1024,1536]{1,0:T(8,128)(2,1)} fusion(bf16[1024,1536]{1,0:T(8,128)(2,1)S(1)} %select_dynamic-update-slice_fusion.refs_1_.refs_3_.refs_5_, bf16[1024,512]{0,1:T(8,128)(2,1)S(1)} %get-tuple-element.46, bf16[1024,512]{0,1:T(8,128)(2,1)S(1)} %get-tuple-element.45), kind=kOutput, calls=%fused_computation | convolution fusion | flops 3226992640 | bytes 8388608 | tf_op jit(solution)/shard_map/dot_general | solution.py:42
  77.2 17.4 %shard_map.67 = (bf16[512,512]{1,0:T(8,128)(2,1)S(1)}, bf16[512,512]{1,0:T(8,128)(2,1)S(1)}, bf16[1024,512]{1,0:T(8,128)(2,1)S(1)}, bf16[1024,512]{1,0:T(8,128)(2,1)S(1)}) custom-call(f32[1,1]{1,0:T(1,128)} %bitcast.bias_ref, bf16[1024,1536]{1,0:T(8,128)(2,1)} %convolution_convert_fusion.q_ref.k_ref.v_ref, ...), custom_call_target="tpu_custom_call" | custom-call | flops 2415919104 | bytes 6291456 | tf_op jit(solution)/shard_map/pallas_call | solution.py:124
  94.6 2.8 %shard_map.68 = bf16[2,512,512]{2,1,0:T(8,128)(2,1)S(1)} custom-call(bf16[1024,512]{1,0:T(8,128)(2,1)S(1)} %get-tuple-element.20.refs_0_.dk_ref.refs_2_, bf16[1024,1536]{1,0:T(8,128)(2,1)} %copy-done, bf16[1024,512]{1,0:T(8,128)(2,1)S(1)} %get-tuple-element.19.refs_2_.dv_ref.refs_4_, bf16[1024,1536]{1,0:T(8,128)(2,1)} %copy-done), custom_call_target="tpu_custom_call" | custom-call | flops 1073741824 | bytes 5242880 | tf_op jit(solution)/shard_map/pallas_call | solution.py:170
  98.2 1.5 fusion.src_ref
  99.7 3.7 %shard_map.69 = bf16[4,256,1024]{2,1,0:T(8,128)(2,1)S(1)} custom-call(bf16[1024,1024]{1,0:T(8,128)(2,1)} %fusion.src_ref, bf16[512,512]{1,0:T(8,128)(2,1)S(1)} %get-tuple-element.23.dq_ref.refs_0_, bf16[1024,512]{1,0:T(8,128)(2,1)S(1)} %get-tuple-element.20.refs_0_.dk_ref.refs_2_, bf16[1024,512]{1,0:T(8,128)(2,1)S(1)} %get-tuple-element.19.refs_2_.dv_ref.refs_4_), custom_call_target="tpu_custom_call" | custom-call | flops 1887436800 | bytes 6291456 | tf_op jit(solution)/shard_map/pallas_call | solution.py:209
  103.4 1.2 dynamic-slice_bitcast_fusion.5
  104.7 4.0 %collective-permute-start.13 = (bf16[512,512]{1,0:T(8,128)(2,1)S(1)}, bf16[512,512]{1,0:T(8,128)(2,1)S(1)}, u32[]{:S(2)}, u32[]{:S(2)}) collective-permute-start(bf16[512,512]{1,0:T(8,128)(2,1)S(1)} %fusion.10), channel_id=1, source_target_pairs={{32,0},{33,1},{36,4},{37,5},{40,8},{41,9},{44,12},{45,13},{48,16},... | collective-permute-start | bytes 1572872 | tf_op jit(solution)/shard_map/ppermute | solution.py:34
  108.8 3.1 %shard_map.70 = bf16[4,1024,256]{2,1,0:T(8,128)(2,1)S(1)} custom-call(bf16[1024,1024]{1,0:T(8,128)(2,1)} %fusion.src_ref, bf16[512,512]{1,0:T(8,128)(2,1)S(1)} %get-tuple-element.23.dq_ref.refs_0_, bf16[1024,512]{1,0:T(8,128)(2,1)S(1)} %get-tuple-element.19.refs_2_.dv_ref.refs_4_, bf16[512,512]{1,0:T(8,128)(2,1)S(1)} %get-tuple-element.22.att_ref, ...), custom_call_target="tpu_custom_call" | custom-call | flops 1342177280 | bytes 6291456 | tf_op jit(solution)/shard_map/pallas_call | solution.py:226
  111.9 1.2 dynamic-slice_bitcast_fusion.1
  113.1 3.7 %shard_map.71 = bf16[2,512,512]{2,1,0:T(8,128)(2,1)S(1)} custom-call(bf16[512,512]{1,0:T(8,128)(2,1)S(1)} %get-tuple-element.23.dq_ref.refs_0_, bf16[1024,1536]{1,0:T(8,128)(2,1)} %copy-done, bf16[1024,512]{1,0:T(8,128)(2,1)S(1)} %get-tuple-element.20.refs_0_.dk_ref.refs_2_, bf16[1024,1536]{1,0:T(8,128)(2,1)} %copy-done, ...), custom_call_target="tpu_custom_call" | custom-call | flops 1610612736 | bytes 5242880 | tf_op jit(solution)/shard_map/pallas_call | solution.py:170
  117.0 4.0 %collective-permute-start.20 = (bf16[1024,256]{1,0:T(8,128)(2,1)}, bf16[1024,256]{1,0:T(8,128)(2,1)S(1)}, u32[]{:S(2)}, u32[]{:S(2)}) collective-permute-start(bf16[1024,256]{1,0:T(8,128)(2,1)} %get-tuple-element.33), channel_id=1, source_target_pairs={{0,2},{1,3},{4,6},{5,7},{8,10},{9,11},{12,14},{13,15},{16,18},{17,... | collective-permute-start | bytes 1572872 | tf_op jit(solution)/shard_map/ppermute | solution.py:34
  121.0 2.0 %collective-permute-start.18 = (bf16[1024,256]{1,0:T(8,128)(2,1)}, bf16[1024,256]{1,0:T(8,128)(2,1)}, u32[]{:S(2)}, u32[]{:S(2)}) collective-permute-start(bf16[1024,256]{1,0:T(8,128)(2,1)} %get-tuple-element.35), channel_id=1, source_target_pairs={{0,32},{1,33},{4,36},{5,37},{8,40},{9,41},{12,44},{13,45},{16,48},... | collective-permute-start | bytes 1572872 | tf_op jit(solution)/shard_map/ppermute | solution.py:34
  123.0 0.6 collective-permute-start.17
  123.7 0.7 collective-permute-start.16
  124.3 1.0 fusion.9
  125.3 7.5 %all-to-all-start.2 = ((bf16[8,64,512]{2,1,0:T(8,128)(2,1)}), bf16[8,64,512]{2,1,0:T(8,128)(2,1)S(1)}, u32[]{:S(2)}, u32[]{:S(2)}) async-start(bf16[8,64,512]{2,1,0:T(8,128)(2,1)} %bitcast.28), calls=%async_computation.2 | async-start | bytes 1048576 | tf_op jit(solution)/shard_map/all_to_all | solution.py:244
  132.8 3.7 %collective-permute-done.20 = bf16[1024,256]{1,0:T(8,128)(2,1)S(1)} collective-permute-done((bf16[1024,256]{1,0:T(8,128)(2,1)}, bf16[1024,256]{1,0:T(8,128)(2,1)S(1)}, u32[]{:S(2)}, u32[]{:S(2)}) %collective-permute-start.20) | collective-permute-done | bytes 524320 | tf_op jit(solution)/shard_map/ppermute | solution.py:34
  136.5 7.8 %collective-permute-done.19 = bf16[1024,256]{1,0:T(8,128)(2,1)} collective-permute-done((bf16[1024,256]{1,0:T(8,128)(2,1)}, bf16[1024,256]{1,0:T(8,128)(2,1)}, u32[]{:S(2)}, u32[]{:S(2)}) %collective-permute-start.19) | collective-permute-done | bytes 524320 | tf_op jit(solution)/shard_map/ppermute | solution.py:34
  144.3 2.6 %collective-permute-done.18 = bf16[1024,256]{1,0:T(8,128)(2,1)} collective-permute-done((bf16[1024,256]{1,0:T(8,128)(2,1)}, bf16[1024,256]{1,0:T(8,128)(2,1)}, u32[]{:S(2)}, u32[]{:S(2)}) %collective-permute-start.18) | collective-permute-done | bytes 524320 | tf_op jit(solution)/shard_map/ppermute | solution.py:34
  146.9 1.5 add_convert_fusion
  148.5 0.7 collective-permute-done.16
  149.2 0.6 collective-permute-done.21
  150.4 1.0 collective-permute-start.23
  151.4 2.2 %collective-permute-start.22 = (bf16[256,256]{1,0:T(8,128)(2,1)S(1)}, bf16[256,256]{1,0:T(8,128)(2,1)}, u32[]{:S(2)}, u32[]{:S(2)}) collective-permute-start(bf16[256,256]{1,0:T(8,128)(2,1)S(1)} %get-tuple-element.64), channel_id=1, source_target_pairs={{0,64},{1,65},{4,68},{5,69},{8,72},{9,73},{12,76},{13,77},{16,80},... | collective-permute-start | bytes 393224 | tf_op jit(solution)/shard_map/ppermute | solution.py:34
  154.4 0.9 copy.34
  155.2 4.2 %all-to-all-start.3 = ((bf16[8,128,256]{2,1,0:T(8,128)(2,1)}), bf16[8,128,256]{2,1,0:T(8,128)(2,1)S(1)}, u32[]{:S(2)}, u32[]{:S(2)}) async-start(bf16[8,128,256]{2,1,0:T(8,128)(2,1)} %bitcast.34), calls=%async_computation.3 | async-start | bytes 1048576 | tf_op jit(solution)/shard_map/all_to_all | solution.py:244
  160.1 1.1 fusion.13
  161.2 8.3 %all-to-all-done.3 = bf16[8,128,256]{2,1,0:T(8,128)(2,1)S(1)} async-done(((bf16[8,128,256]{2,1,0:T(8,128)(2,1)}), bf16[8,128,256]{2,1,0:T(8,128)(2,1)S(1)}, u32[]{:S(2)}, u32[]{:S(2)}) %all-to-all-start.3) | async-done | bytes 524320 | tf_op jit(solution)/shard_map/all_to_all | solution.py:244
  169.6 0.7 copy.35
  170.4 7.2 %all-to-all-start.4 = ((bf16[8,4,16,256]{3,2,1,0:T(8,128)(2,1)}), bf16[8,4,16,256]{3,2,1,0:T(8,128)(2,1)S(1)}, u32[]{:S(2)}, u32[]{:S(2)}) async-start(bf16[8,4,16,256]{3,2,1,0:T(8,128)(2,1)} %copy.35), calls=%async_computation.4 | async-start | bytes 524288 | tf_op jit(solution)/shard_map/all_to_all | solution.py:244
  177.7 0.9 maximum_bitcast_fusion
  178.5 10.3 %all-to-all-done.4 = bf16[8,4,16,256]{3,2,1,0:T(8,128)(2,1)S(1)} async-done(((bf16[8,4,16,256]{3,2,1,0:T(8,128)(2,1)}), bf16[8,4,16,256]{3,2,1,0:T(8,128)(2,1)S(1)}, u32[]{:S(2)}, u32[]{:S(2)}) %all-to-all-start.4) | async-done | bytes 262176 | tf_op jit(solution)/shard_map/all_to_all | solution.py:244
  (79 shorter events, 8.0 us)
Async XLA Ops:
  0.6 7.2 %copy-start.1 = (bf16[1024,768]{1,0:T(8,128)(2,1)S(1)}, bf16[1024,768]{1,0:T(8,128)(2,1)}, u32[]{:S(2)}) copy-start(bf16[1024,768]{1,0:T(8,128)(2,1)} %param.6) | copy-start | bytes 4718596
  0.6 5.8 %copy-start.2 = (bf16[1,4,64,1024]{3,2,1,0:T(8,128)(2,1)S(1)}, bf16[1,4,64,1024]{3,2,1,0:T(8,128)(2,1)}, u32[]{:S(2)}) copy-start(bf16[1,4,64,1024]{3,2,1,0:T(8,128)(2,1)} %param.4) | copy-start | bytes 1572868
  0.7 5.9 %copy-start.3 = (bf16[1,4,64,1024]{3,2,1,0:T(8,128)(2,1)S(1)}, bf16[1,4,64,1024]{3,2,1,0:T(8,128)(2,1)}, u32[]{:S(2)}) copy-start(bf16[1,4,64,1024]{3,2,1,0:T(8,128)(2,1)} %param.5) | copy-start | bytes 1572868
  3.7 15.4 %collective-permute-start.3 = (bf16[256,1024]{1,0:T(8,128)(2,1)}, bf16[256,1024]{1,0:T(8,128)(2,1)}, u32[]{:S(2)}, u32[]{:S(2)}) collective-permute-start(bf16[256,1024]{1,0:T(8,128)(2,1)} %pad_maximum_fusion.9), channel_id=1, source_target_pairs={{0,34},{1,35},{4,38},{5,39},{8,42},{9,43},{12,46},{13,47},{16,50},... | collective-permute-start | bytes 1572872 | tf_op jit(solution)/shard_map/ppermute | solution.py:34
  6.5 2.5 %collective-permute-start = (bf16[4,64,512]{2,1,0:T(8,128)(2,1)S(1)}, bf16[4,64,512]{2,1,0:T(8,128)(2,1)S(1)}, u32[]{:S(2)}, u32[]{:S(2)}) collective-permute-start(bf16[4,64,512]{2,1,0:T(8,128)(2,1)S(1)} %broadcast_select_fusion.18), channel_id=1, source_target_pairs={{0,1},{1,0},{4,5},{5,4},{8,9},{9,8},{12,13},{13,12},{16,17},{17,16... | collective-permute-start | bytes 786440 | tf_op jit(solution)/shard_map/ppermute | solution.py:34
  7.3 16.0 %collective-permute-start.9 = (bf16[4,64,512]{2,1,0:T(8,128)(2,1)}, bf16[4,64,512]{2,1,0:T(8,128)(2,1)}, u32[]{:S(2)}, u32[]{:S(2)}) collective-permute-start(bf16[4,64,512]{2,1,0:T(8,128)(2,1)} %broadcast_select_fusion.14), channel_id=1, source_target_pairs={{0,1},{1,0},{4,5},{5,4},{8,9},{9,8},{12,13},{13,12},{16,17},{17,16... | collective-permute-start | bytes 786440 | tf_op jit(solution)/shard_map/ppermute | solution.py:34
  9.0 9.4 %copy-start.7 = (bf16[1024,256]{1,0:T(8,128)(2,1)S(1)}, bf16[1024,256]{1,0:T(8,128)(2,1)}, u32[]{:S(2)}) copy-start(bf16[1024,256]{1,0:T(8,128)(2,1)} %param.7) | copy-start | bytes 1572868
  9.0 10.3 %copy-start.4 = (bf16[1024,256]{1,0:T(8,128)(2,1)S(1)}, bf16[1024,256]{1,0:T(8,128)(2,1)}, u32[]{:S(2)}) copy-start(bf16[1024,256]{1,0:T(8,128)(2,1)} %get-tuple-element.55) | copy-start | bytes 1572868
  9.9 26.1 %all-to-all-start = ((bf16[8,64,512]{2,1,0:T(8,128)(2,1)}), bf16[8,64,512]{2,1,0:T(8,128)(2,1)S(1)}, u32[]{:S(2)}, u32[]{:S(2)}) async-start(bf16[8,64,512]{2,1,0:T(8,128)(2,1)} %pad_maximum_fusion.8), calls=%async_computation | async-start | bytes 1048576 | tf_op jit(solution)/shard_map/all_to_all | solution.py:244
  19.1 15.1 %collective-permute-start.4 = (bf16[256,1024]{1,0:T(8,128)(2,1)}, bf16[256,1024]{1,0:T(8,128)(2,1)}, u32[]{:S(2)}, u32[]{:S(2)}) collective-permute-start(bf16[256,1024]{1,0:T(8,128)(2,1)} %collective-permute-done.3), channel_id=1, source_target_pairs={{0,64},{1,65},{4,68},{5,69},{8,72},{9,73},{12,76},{13,77},{16,80},... | collective-permute-start | bytes 1572872 | tf_op jit(solution)/shard_map/ppermute | solution.py:34
  20.3 47.2 %collective-permute-start.7 = (bf16[1536,256]{1,0:T(8,128)(2,1)}, bf16[1536,256]{1,0:T(8,128)(2,1)}, u32[]{:S(2)}, u32[]{:S(2)}) collective-permute-start(bf16[1536,256]{1,0:T(8,128)(2,1)} %pad_maximum_fusion.6), channel_id=1, source_target_pairs={{0,1},{1,0},{4,5},{5,4},{8,9},{9,8},{12,13},{13,12},{16,17},{17,16... | collective-permute-start | bytes 2359304 | tf_op jit(solution)/shard_map/ppermute | solution.py:34
  20.3 27.1 %collective-permute-start.5 = (bf16[256,1024]{1,0:T(8,128)(2,1)}, bf16[256,1024]{1,0:T(8,128)(2,1)}, u32[]{:S(2)}, u32[]{:S(2)}) collective-permute-start(bf16[256,1024]{1,0:T(8,128)(2,1)} %collective-permute-done.3), channel_id=1, source_target_pairs={{0,192},{1,193},{4,196},{5,197},{8,200},{9,201},{12,204},{13,205},... | collective-permute-start | bytes 1572872 | tf_op jit(solution)/shard_map/ppermute | solution.py:34
  22.1 26.4 %collective-permute-start.6 = (bf16[256,1024]{1,0:T(8,128)(2,1)}, bf16[256,1024]{1,0:T(8,128)(2,1)}, u32[]{:S(2)}, u32[]{:S(2)}) collective-permute-start(bf16[256,1024]{1,0:T(8,128)(2,1)} %collective-permute-done.3), channel_id=1, source_target_pairs={{0,128},{1,129},{4,132},{5,133},{8,136},{9,137},{12,140},{13,141},... | collective-permute-start | bytes 1572872 | tf_op jit(solution)/shard_map/ppermute | solution.py:34
  36.0 21.5 %all-to-all-start.1 = ((bf16[8,64,512]{2,1,0:T(8,128)(2,1)}), bf16[8,64,512]{2,1,0:T(8,128)(2,1)S(1)}, u32[]{:S(2)}, u32[]{:S(2)}) async-start(bf16[8,64,512]{2,1,0:T(8,128)(2,1)} %pad_maximum_fusion.10), calls=%async_computation.1 | async-start | bytes 1048576 | tf_op jit(solution)/shard_map/all_to_all | solution.py:244
  50.7 3.2 %copy-start.5 = (bf16[1024,256]{1,0:T(8,128)(2,1)S(1)}, bf16[1024,256]{1,0:T(8,128)(2,1)}, u32[]{:S(2)}) copy-start(bf16[1024,256]{1,0:T(8,128)(2,1)} %get-tuple-element.48) | copy-start | bytes 1572868
  50.7 6.8 %copy-start.6 = (bf16[1024,256]{1,0:T(8,128)(2,1)S(1)}, bf16[1024,256]{1,0:T(8,128)(2,1)}, u32[]{:S(2)}) copy-start(bf16[1024,256]{1,0:T(8,128)(2,1)} %get-tuple-element.53) | copy-start | bytes 1572868
  51.8 15.1 %collective-permute-start.1 = (bf16[512,512]{0,1:T(8,128)(2,1)S(1)}, bf16[512,512]{0,1:T(8,128)(2,1)S(1)}, u32[]{:S(2)}, u32[]{:S(2)}) collective-permute-start(bf16[512,512]{0,1:T(8,128)(2,1)S(1)} %copy.32), channel_id=1, source_target_pairs={{0,32},{1,33},{4,36},{5,37},{8,40},{9,41},{12,44},{13,45},{16,48},... | collective-permute-start | bytes 1572872 | tf_op jit(solution)/shard_map/ppermute | solution.py:34
  55.0 12.5 %collective-permute-start.8 = (bf16[1536,256]{1,0:T(8,128)(2,1)S(1)}, bf16[1536,256]{1,0:T(8,128)(2,1)}, u32[]{:S(2)}, u32[]{:S(2)}) collective-permute-start(bf16[1536,256]{1,0:T(8,128)(2,1)S(1)} %pad_maximum_fusion.7), channel_id=1, source_target_pairs={{0,1},{1,0},{4,5},{5,4},{8,9},{9,8},{12,13},{13,12},{16,17},{17,16... | collective-permute-start | bytes 2359304 | tf_op jit(solution)/shard_map/ppermute | solution.py:34
  57.6 9.8 %collective-permute-start.10 = (bf16[512,512]{1,0:T(8,128)(2,1)S(1)}, bf16[512,512]{1,0:T(8,128)(2,1)S(1)}, u32[]{:S(2)}, u32[]{:S(2)}) collective-permute-start(bf16[512,512]{1,0:T(8,128)(2,1)S(1)} %bitcast.107), channel_id=1, source_target_pairs={{0,1},{1,0},{4,5},{5,4},{8,9},{9,8},{12,13},{13,12},{16,17},{17,16... | collective-permute-start | bytes 1572872 | tf_op jit(solution)/shard_map/ppermute | solution.py:34
  67.0 3.7 %collective-permute-start.2 = (bf16[1024,512]{0,1:T(8,128)(2,1)S(1)}, bf16[1024,512]{0,1:T(8,128)(2,1)S(1)}, u32[]{:S(2)}, u32[]{:S(2)}) collective-permute-start(bf16[1024,512]{0,1:T(8,128)(2,1)S(1)} %pad_maximum_fusion.4), channel_id=1, source_target_pairs={{0,1},{1,0},{4,5},{5,4},{8,9},{9,8},{12,13},{13,12},{16,17},{17,16... | collective-permute-start | bytes 3145736 | tf_op jit(solution)/shard_map/ppermute | solution.py:34
  70.7 1.6 copy-start
  97.5 7.1 %collective-permute-start.11 = (bf16[512,512]{1,0:T(8,128)(2,1)S(1)}, bf16[512,512]{1,0:T(8,128)(2,1)S(1)}, u32[]{:S(2)}, u32[]{:S(2)}) collective-permute-start(bf16[512,512]{1,0:T(8,128)(2,1)S(1)} %dynamic-slice_bitcast_fusion.9), channel_id=1, source_target_pairs={{0,1},{1,0},{4,5},{5,4},{8,9},{9,8},{12,13},{13,12},{16,17},{17,16... | collective-permute-start | bytes 1572872 | tf_op jit(solution)/shard_map/ppermute | solution.py:34
  104.7 18.3 %collective-permute-start.13 = (bf16[512,512]{1,0:T(8,128)(2,1)S(1)}, bf16[512,512]{1,0:T(8,128)(2,1)S(1)}, u32[]{:S(2)}, u32[]{:S(2)}) collective-permute-start(bf16[512,512]{1,0:T(8,128)(2,1)S(1)} %fusion.10), channel_id=1, source_target_pairs={{32,0},{33,1},{36,4},{37,5},{40,8},{41,9},{44,12},{45,13},{48,16},... | collective-permute-start | bytes 1572872 | tf_op jit(solution)/shard_map/ppermute | solution.py:34
  116.9 6.8 %collective-permute-start.12 = (bf16[512,512]{1,0:T(8,128)(2,1)S(1)}, bf16[512,512]{1,0:T(8,128)(2,1)S(1)}, u32[]{:S(2)}, u32[]{:S(2)}) collective-permute-start(bf16[512,512]{1,0:T(8,128)(2,1)S(1)} %dynamic-slice_bitcast_fusion), channel_id=1, source_target_pairs={{0,1},{1,0},{4,5},{5,4},{8,9},{9,8},{12,13},{13,12},{16,17},{17,16... | collective-permute-start | bytes 1572872 | tf_op jit(solution)/shard_map/ppermute | solution.py:34
  117.0 19.5 %collective-permute-start.20 = (bf16[1024,256]{1,0:T(8,128)(2,1)}, bf16[1024,256]{1,0:T(8,128)(2,1)S(1)}, u32[]{:S(2)}, u32[]{:S(2)}) collective-permute-start(bf16[1024,256]{1,0:T(8,128)(2,1)} %get-tuple-element.33), channel_id=1, source_target_pairs={{0,2},{1,3},{4,6},{5,7},{8,10},{9,11},{12,14},{13,15},{16,18},{17,... | collective-permute-start | bytes 1572872 | tf_op jit(solution)/shard_map/ppermute | solution.py:34
  121.0 23.3 %collective-permute-start.19 = (bf16[1024,256]{1,0:T(8,128)(2,1)}, bf16[1024,256]{1,0:T(8,128)(2,1)}, u32[]{:S(2)}, u32[]{:S(2)}) collective-permute-start(bf16[1024,256]{1,0:T(8,128)(2,1)} %get-tuple-element.34), channel_id=1, source_target_pairs={{0,34},{1,35},{4,38},{5,39},{8,42},{9,43},{12,46},{13,47},{16,50},... | collective-permute-start | bytes 1572872 | tf_op jit(solution)/shard_map/ppermute | solution.py:34
  121.0 25.9 %collective-permute-start.18 = (bf16[1024,256]{1,0:T(8,128)(2,1)}, bf16[1024,256]{1,0:T(8,128)(2,1)}, u32[]{:S(2)}, u32[]{:S(2)}) collective-permute-start(bf16[1024,256]{1,0:T(8,128)(2,1)} %get-tuple-element.35), channel_id=1, source_target_pairs={{0,32},{1,33},{4,36},{5,37},{8,40},{9,41},{12,44},{13,45},{16,48},... | collective-permute-start | bytes 1572872 | tf_op jit(solution)/shard_map/ppermute | solution.py:34
  123.0 25.5 %collective-permute-start.17 = (bf16[256,1024]{1,0:T(8,128)(2,1)}, bf16[256,1024]{1,0:T(8,128)(2,1)S(1)}, u32[]{:S(2)}, u32[]{:S(2)}) collective-permute-start(bf16[256,1024]{1,0:T(8,128)(2,1)} %get-tuple-element.37), channel_id=1, source_target_pairs={{0,128},{1,129},{4,132},{5,133},{8,136},{9,137},{12,140},{13,141},... | collective-permute-start | bytes 1572872 | tf_op jit(solution)/shard_map/ppermute | solution.py:34
  123.7 25.5 %collective-permute-start.16 = (bf16[256,1024]{1,0:T(8,128)(2,1)}, bf16[256,1024]{1,0:T(8,128)(2,1)S(1)}, u32[]{:S(2)}, u32[]{:S(2)}) collective-permute-start(bf16[256,1024]{1,0:T(8,128)(2,1)} %get-tuple-element.38), channel_id=1, source_target_pairs={{0,192},{1,193},{4,196},{5,197},{8,200},{9,201},{12,204},{13,205},... | collective-permute-start | bytes 1572872 | tf_op jit(solution)/shard_map/ppermute | solution.py:34
  125.3 28.7 %all-to-all-start.2 = ((bf16[8,64,512]{2,1,0:T(8,128)(2,1)}), bf16[8,64,512]{2,1,0:T(8,128)(2,1)S(1)}, u32[]{:S(2)}, u32[]{:S(2)}) async-start(bf16[8,64,512]{2,1,0:T(8,128)(2,1)} %bitcast.28), calls=%async_computation.2 | async-start | bytes 1048576 | tf_op jit(solution)/shard_map/all_to_all | solution.py:244
  136.5 12.7 %collective-permute-start.15 = (bf16[256,1024]{1,0:T(8,128)(2,1)}, bf16[256,1024]{1,0:T(8,128)(2,1)S(1)}, u32[]{:S(2)}, u32[]{:S(2)}) collective-permute-start(bf16[256,1024]{1,0:T(8,128)(2,1)} %get-tuple-element.39), channel_id=1, source_target_pairs={{0,64},{1,65},{4,68},{5,69},{8,72},{9,73},{12,76},{13,77},{16,80},... | collective-permute-start | bytes 1572872 | tf_op jit(solution)/shard_map/ppermute | solution.py:34
  148.4 1.4 collective-permute-start.21
  150.0 9.5 %collective-permute-start.24 = (bf16[256,256]{1,0:T(8,128)(2,1)S(1)}, bf16[256,256]{1,0:T(8,128)(2,1)}, u32[]{:S(2)}, u32[]{:S(2)}) collective-permute-start(bf16[256,256]{1,0:T(8,128)(2,1)S(1)} %get-tuple-element.66), channel_id=1, source_target_pairs={{0,128},{1,129},{4,132},{5,133},{8,136},{9,137},{12,140},{13,141},... | collective-permute-start | bytes 393224 | tf_op jit(solution)/shard_map/ppermute | solution.py:34
  150.4 9.4 %collective-permute-start.23 = (bf16[256,256]{1,0:T(8,128)(2,1)S(1)}, bf16[256,256]{1,0:T(8,128)(2,1)}, u32[]{:S(2)}, u32[]{:S(2)}) collective-permute-start(bf16[256,256]{1,0:T(8,128)(2,1)S(1)} %get-tuple-element.65), channel_id=1, source_target_pairs={{0,192},{1,193},{4,196},{5,197},{8,200},{9,201},{12,204},{13,205},... | collective-permute-start | bytes 393224 | tf_op jit(solution)/shard_map/ppermute | solution.py:34
  151.4 8.4 %collective-permute-start.22 = (bf16[256,256]{1,0:T(8,128)(2,1)S(1)}, bf16[256,256]{1,0:T(8,128)(2,1)}, u32[]{:S(2)}, u32[]{:S(2)}) collective-permute-start(bf16[256,256]{1,0:T(8,128)(2,1)S(1)} %get-tuple-element.64), channel_id=1, source_target_pairs={{0,64},{1,65},{4,68},{5,69},{8,72},{9,73},{12,76},{13,77},{16,80},... | collective-permute-start | bytes 393224 | tf_op jit(solution)/shard_map/ppermute | solution.py:34
  155.2 14.3 %all-to-all-start.3 = ((bf16[8,128,256]{2,1,0:T(8,128)(2,1)}), bf16[8,128,256]{2,1,0:T(8,128)(2,1)S(1)}, u32[]{:S(2)}, u32[]{:S(2)}) async-start(bf16[8,128,256]{2,1,0:T(8,128)(2,1)} %bitcast.34), calls=%async_computation.3 | async-start | bytes 1048576 | tf_op jit(solution)/shard_map/all_to_all | solution.py:244
  159.8 17.8 %collective-permute-start.14 = (bf16[4,64,512]{2,1,0:T(8,128)(2,1)S(1)}, bf16[4,64,512]{2,1,0:T(8,128)(2,1)S(1)}, u32[]{:S(2)}, u32[]{:S(2)}) collective-permute-start(bf16[4,64,512]{2,1,0:T(8,128)(2,1)S(1)} %dynamic-slice_bitcast_fusion.10), channel_id=1, source_target_pairs={{0,1},{1,0},{4,5},{5,4},{8,9},{9,8},{12,13},{13,12},{16,17},{17,16... | collective-permute-start | bytes 786440 | tf_op jit(solution)/shard_map/ppermute | solution.py:34
  170.4 18.5 %all-to-all-start.4 = ((bf16[8,4,16,256]{3,2,1,0:T(8,128)(2,1)}), bf16[8,4,16,256]{3,2,1,0:T(8,128)(2,1)S(1)}, u32[]{:S(2)}, u32[]{:S(2)}) async-start(bf16[8,4,16,256]{3,2,1,0:T(8,128)(2,1)} %copy.35), calls=%async_computation.4 | async-start | bytes 524288 | tf_op jit(solution)/shard_map/all_to_all | solution.py:244
